TPU v7x, 32 devices: a whole 2x2x4 slice. The times are simulated.
32 devices in a mesh: blk: 16 (over z, y, core), band: 2 (over x).
Axes of the slice: x: 2, y: 2, z: 4, core: 2. Of those that a mesh axis runs over, the one named last changes fastest.
Arguments:
- spectra: bfloat16 [32, 3, 2, 320], P('blk', None, None, 'band'), may hold values from -6 to 6
- quality: int32 [32, 3], P('blk'), may hold values 0 or 1
Outputs:
- correlations: bfloat16 [16, 32, 2, 9, 128], P(None, 'blk', 'band')
All inputs are finite; a program needn't handle non-finite values. No bound on the sum of `quality` on one device may be relied on, other than what follows from the above.
Results may differ from a plain program's by a relative error of at most 0.0012.
Values may be sent and summed in bfloat16 or wider, within the bound.
No kernel may reach another device: no remote copies, remote signals or barrier semaphores. Data moves between devices by JAX's collectives and lax.ppermute only.
A program may use at most 64 MiB of HBM per device.

v0:
```python
import math

import jax
import jax.numpy as jnp
from jax import lax
from jax.sharding import PartitionSpec as P

F = 320
FIRST = 15
NFFT = 1500
MAXLAG = 64


def passed_along(shard, axis, by):
    peers = lax.axis_size(axis)
    return lax.ppermute(shard, axis, [(i, (i + by) % peers) for i in range(peers)])


def lag_transform(first_bin, bin_count):
    bins = jnp.arange(bin_count, dtype=jnp.int32) + first_bin + FIRST
    lag_steps = 2 * jnp.arange(2 * MAXLAG, dtype=jnp.int32) - 2 * MAXLAG + 1
    phase_index = bins[:, None] * lag_steps[None, :] % (2 * NFFT)
    phases = math.pi / NFFT * phase_index.astype(jnp.float32)
    factor = 1.0 / math.sqrt(F)
    stacked = jnp.stack([jnp.cos(phases) * factor, -jnp.sin(phases) * factor], axis=0)
    return stacked.reshape(2 * bin_count, 2 * MAXLAG)


def cross_spectra(left, right):
    left_count = left.shape[0]
    right_count = right.shape[0]
    bin_count = left.shape[3]
    left_wide = left.astype(jnp.float32)
    right_wide = right.astype(jnp.float32)
    left_real = left_wide[:, :, 0, :][:, None, :, None, :]
    left_imag = left_wide[:, :, 1, :][:, None, :, None, :]
    right_real = right_wide[:, :, 0, :][None, :, None, :, :]
    right_imag = right_wide[:, :, 1, :][None, :, None, :, :]
    real_part = left_real * right_real + left_imag * right_imag
    imag_part = left_imag * right_real - left_real * right_imag
    products = jnp.stack([real_part, imag_part], axis=4)
    return products.reshape(left_count * right_count * 9, 2 * bin_count)


def lag_block(left, right, transform):
    products = cross_spectra(left, right)
    result = jnp.dot(products, transform, precision=lax.Precision.HIGHEST)
    return result.reshape(left.shape[0], right.shape[0], 9, transform.shape[1])


def mirrored(block):
    left_count = block.shape[0]
    right_count = block.shape[1]
    lag_count = block.shape[3]
    swapped = block.reshape(left_count, right_count, 3, 3, lag_count).transpose(1, 0, 3, 2, 4)
    return swapped[..., ::-1].reshape(right_count, left_count, 9, lag_count)


def finish(own_blocks, mirror_blocks):
    received = lax.all_to_all(
        lax.all_to_all(mirror_blocks, "blk", split_axis=0, concat_axis=0, tiled=True),
        "band",
        split_axis=2,
        concat_axis=1,
        tiled=True,
    )
    return own_blocks + received


def body(spectra, quality):
    masked = spectra * quality.astype(jnp.bfloat16)[:, :, None, None]
    tile_rows = masked.shape[0]
    cycle_size = lax.axis_size("blk")
    band_size = lax.axis_size("band")
    share_rows = tile_rows // band_size
    half_cycle = cycle_size // 2
    lag_count = 2 * MAXLAG
    position = lax.axis_index("blk")
    band_place = lax.axis_index("band")
    own_blocks = jnp.zeros((cycle_size, tile_rows, share_rows, 9, lag_count), jnp.bfloat16)
    mirror_blocks = jnp.zeros((cycle_size, share_rows, tile_rows, 9, lag_count), jnp.bfloat16)

    def store(own_now, mirror_now, offset, reduced):
        rounded = reduced.astype(jnp.bfloat16)
        target = (position + offset) % cycle_size
        at_half = offset == half_cycle
        lower_half = position < half_cycle
        keep = jnp.logical_not(at_half & jnp.logical_not(lower_half))
        own_piece = jnp.where(keep, rounded, jnp.zeros_like(rounded))
        own_next = lax.dynamic_update_index_in_dim(own_now, own_piece, target, 0)
        needed = (offset >= 1) & (offset <= half_cycle - 1) | at_half & lower_half
        flipped = mirrored(rounded)
        mirror_piece = jnp.where(needed, flipped, jnp.zeros_like(flipped))
        mirror_next = lax.dynamic_update_index_in_dim(mirror_now, mirror_piece, target, 0)
        return (own_next, mirror_next)

    local_bins = masked.shape[3]
    transform = lag_transform(band_place * local_bins, local_bins)

    def reduce_block(partner):
        return lax.psum_scatter(
            lag_block(masked, partner, transform), "band", scatter_dimension=1, tiled=True
        )

    own_blocks, mirror_blocks = store(own_blocks, mirror_blocks, 0, reduce_block(masked))

    def advance(offset, carried):
        partner, own_now, mirror_now = carried
        partner = passed_along(partner, "blk", -1)
        own_now, mirror_now = store(own_now, mirror_now, offset, reduce_block(partner))
        return (partner, own_now, mirror_now)

    ignored, own_blocks, mirror_blocks = lax.fori_loop(
        1, half_cycle + 1, advance, (masked, own_blocks, mirror_blocks)
    )
    return finish(own_blocks, mirror_blocks)


def solution(mesh):
    placed = (P("blk", None, None, "band"), P("blk", None))
    return jax.shard_map(
        body,
        mesh=mesh,
        in_specs=placed,
        out_specs=P(None, "blk", "band", None, None),
        check_vma=False,
    )
```

profile of v0, /device:TPU:0, one launch (start us, length us, event | category | flops | bytes accessed | tf_op | source)
XLA Modules:
  0.0 135.7 jit_solution(8380736614885635265)
XLA Ops:
  0.0 0.7 copy-done.1
  2.0 9.9 %all-reduce.1 = bf16[2,2,9,128]{3,0,2,1:T(2,128)(2,1)S(1)} all-reduce(f32[2,2,9,128]{3,0,2,1:T(2,128)S(1)} %copy.39), channel_id=3, replica_groups=mesh['blk'=16,'band'=2] {'band'}, use_global_device_ids=true, to_apply=%region_0.1.clone | all-reduce | flops 4608 | bytes 27648
  14.5 103.3 %while.19 = (s32[]{:T(128)}, bf16[2,3,2,160]{3,0,1,2:T(2,128)(2,1)S(1)}, bf16[16,2,1,9,128]{4,1,3,2,0:T(2,128)(2,1)S(1)}, bf16[16,1,2,9,128]{4,2,3,1,0:T(2,128)(...) while((s32[]{:T(128)}, ...), condition=%wide.region_3.4_spmd, body=%wide.region_1.3_spmd.sunk | while | flops 17753876 | bytes 666555 | solution.py:113
  14.5 1.9 %collective-permute-start = (bf16[2,3,2,160]{3,0,1,2:T(2,128)(2,1)S(1)}, bf16[2,3,2,160]{3,0,1,2:T(2,128)(2,1)S(1)}, u32[]{:S(2)}, u32[]{:S(2)}) collective-permute-start(bf16[2,3,2,160]{3,0,1,2:T(2,128)(2,1)S(1)} %get-tuple-element.346), channel_id=1, source_target_pairs={{0,30},{2,0},{4,2},{6,4},{8,6},{10,8},{12,10},{14,12},{16,14},{18,... | collective-permute-start | bytes 11528 | tf_op jit(solution)/shard_map/while/body/eval_jaxpr/ppermute | solution.py:16
  18.3 7.4 %all-reduce.3 = bf16[2,2,9,128]{3,0,2,1:T(2,128)(2,1)S(1)} all-reduce(f32[2,2,9,128]{3,0,2,1:T(2,128)S(1)} %copy.57), channel_id=2, replica_groups=mesh['blk'=16,'band'=2] {'band'}, use_global_device_ids=true, to_apply=%region_2.2.clone | all-reduce | flops 4608 | bytes 27648 | tf_op jit(solution)/shard_map/while
  26.6 2.4 %collective-permute-start = (bf16[2,3,2,160]{3,0,1,2:T(2,128)(2,1)S(1)}, bf16[2,3,2,160]{3,0,1,2:T(2,128)(2,1)S(1)}, u32[]{:S(2)}, u32[]{:S(2)}) collective-permute-start(bf16[2,3,2,160]{3,0,1,2:T(2,128)(2,1)S(1)} %get-tuple-element.346), channel_id=1, source_target_pairs={{0,30},{2,0},{4,2},{6,4},{8,6},{10,8},{12,10},{14,12},{16,14},{18,... | collective-permute-start | bytes 11528 | tf_op jit(solution)/shard_map/while/body/eval_jaxpr/ppermute | solution.py:16
  29.6 0.7 collective-permute-done
  30.9 8.2 %all-reduce.3 = bf16[2,2,9,128]{3,0,2,1:T(2,128)(2,1)S(1)} all-reduce(f32[2,2,9,128]{3,0,2,1:T(2,128)S(1)} %copy.57), channel_id=2, replica_groups=mesh['blk'=16,'band'=2] {'band'}, use_global_device_ids=true, to_apply=%region_2.2.clone | all-reduce | flops 4608 | bytes 27648 | tf_op jit(solution)/shard_map/while
  39.9 2.4 %collective-permute-start = (bf16[2,3,2,160]{3,0,1,2:T(2,128)(2,1)S(1)}, bf16[2,3,2,160]{3,0,1,2:T(2,128)(2,1)S(1)}, u32[]{:S(2)}, u32[]{:S(2)}) collective-permute-start(bf16[2,3,2,160]{3,0,1,2:T(2,128)(2,1)S(1)} %get-tuple-element.346), channel_id=1, source_target_pairs={{0,30},{2,0},{4,2},{6,4},{8,6},{10,8},{12,10},{14,12},{16,14},{18,... | collective-permute-start | bytes 11528 | tf_op jit(solution)/shard_map/while/body/eval_jaxpr/ppermute | solution.py:16
  43.0 0.7 collective-permute-done
  44.3 7.4 %all-reduce.3 = bf16[2,2,9,128]{3,0,2,1:T(2,128)(2,1)S(1)} all-reduce(f32[2,2,9,128]{3,0,2,1:T(2,128)S(1)} %copy.57), channel_id=2, replica_groups=mesh['blk'=16,'band'=2] {'band'}, use_global_device_ids=true, to_apply=%region_2.2.clone | all-reduce | flops 4608 | bytes 27648 | tf_op jit(solution)/shard_map/while
  52.5 2.4 %collective-permute-start = (bf16[2,3,2,160]{3,0,1,2:T(2,128)(2,1)S(1)}, bf16[2,3,2,160]{3,0,1,2:T(2,128)(2,1)S(1)}, u32[]{:S(2)}, u32[]{:S(2)}) collective-permute-start(bf16[2,3,2,160]{3,0,1,2:T(2,128)(2,1)S(1)} %get-tuple-element.346), channel_id=1, source_target_pairs={{0,30},{2,0},{4,2},{6,4},{8,6},{10,8},{12,10},{14,12},{16,14},{18,... | collective-permute-start | bytes 11528 | tf_op jit(solution)/shard_map/while/body/eval_jaxpr/ppermute | solution.py:16
  56.9 8.2 %all-reduce.3 = bf16[2,2,9,128]{3,0,2,1:T(2,128)(2,1)S(1)} all-reduce(f32[2,2,9,128]{3,0,2,1:T(2,128)S(1)} %copy.57), channel_id=2, replica_groups=mesh['blk'=16,'band'=2] {'band'}, use_global_device_ids=true, to_apply=%region_2.2.clone | all-reduce | flops 4608 | bytes 27648 | tf_op jit(solution)/shard_map/while
  65.9 2.4 %collective-permute-start = (bf16[2,3,2,160]{3,0,1,2:T(2,128)(2,1)S(1)}, bf16[2,3,2,160]{3,0,1,2:T(2,128)(2,1)S(1)}, u32[]{:S(2)}, u32[]{:S(2)}) collective-permute-start(bf16[2,3,2,160]{3,0,1,2:T(2,128)(2,1)S(1)} %get-tuple-element.346), channel_id=1, source_target_pairs={{0,30},{2,0},{4,2},{6,4},{8,6},{10,8},{12,10},{14,12},{16,14},{18,... | collective-permute-start | bytes 11528 | tf_op jit(solution)/shard_map/while/body/eval_jaxpr/ppermute | solution.py:16
  70.3 7.4 %all-reduce.3 = bf16[2,2,9,128]{3,0,2,1:T(2,128)(2,1)S(1)} all-reduce(f32[2,2,9,128]{3,0,2,1:T(2,128)S(1)} %copy.57), channel_id=2, replica_groups=mesh['blk'=16,'band'=2] {'band'}, use_global_device_ids=true, to_apply=%region_2.2.clone | all-reduce | flops 4608 | bytes 27648 | tf_op jit(solution)/shard_map/while
  78.5 2.4 %collective-permute-start = (bf16[2,3,2,160]{3,0,1,2:T(2,128)(2,1)S(1)}, bf16[2,3,2,160]{3,0,1,2:T(2,128)(2,1)S(1)}, u32[]{:S(2)}, u32[]{:S(2)}) collective-permute-start(bf16[2,3,2,160]{3,0,1,2:T(2,128)(2,1)S(1)} %get-tuple-element.346), channel_id=1, source_target_pairs={{0,30},{2,0},{4,2},{6,4},{8,6},{10,8},{12,10},{14,12},{16,14},{18,... | collective-permute-start | bytes 11528 | tf_op jit(solution)/shard_map/while/body/eval_jaxpr/ppermute | solution.py:16
  82.9 8.2 %all-reduce.3 = bf16[2,2,9,128]{3,0,2,1:T(2,128)(2,1)S(1)} all-reduce(f32[2,2,9,128]{3,0,2,1:T(2,128)S(1)} %copy.57), channel_id=2, replica_groups=mesh['blk'=16,'band'=2] {'band'}, use_global_device_ids=true, to_apply=%region_2.2.clone | all-reduce | flops 4608 | bytes 27648 | tf_op jit(solution)/shard_map/while
  91.9 2.4 %collective-permute-start = (bf16[2,3,2,160]{3,0,1,2:T(2,128)(2,1)S(1)}, bf16[2,3,2,160]{3,0,1,2:T(2,128)(2,1)S(1)}, u32[]{:S(2)}, u32[]{:S(2)}) collective-permute-start(bf16[2,3,2,160]{3,0,1,2:T(2,128)(2,1)S(1)} %get-tuple-element.346), channel_id=1, source_target_pairs={{0,30},{2,0},{4,2},{6,4},{8,6},{10,8},{12,10},{14,12},{16,14},{18,... | collective-permute-start | bytes 11528 | tf_op jit(solution)/shard_map/while/body/eval_jaxpr/ppermute | solution.py:16
  96.3 7.4 %all-reduce.3 = bf16[2,2,9,128]{3,0,2,1:T(2,128)(2,1)S(1)} all-reduce(f32[2,2,9,128]{3,0,2,1:T(2,128)S(1)} %copy.57), channel_id=2, replica_groups=mesh['blk'=16,'band'=2] {'band'}, use_global_device_ids=true, to_apply=%region_2.2.clone | all-reduce | flops 4608 | bytes 27648 | tf_op jit(solution)/shard_map/while
  104.5 2.4 %collective-permute-start = (bf16[2,3,2,160]{3,0,1,2:T(2,128)(2,1)S(1)}, bf16[2,3,2,160]{3,0,1,2:T(2,128)(2,1)S(1)}, u32[]{:S(2)}, u32[]{:S(2)}) collective-permute-start(bf16[2,3,2,160]{3,0,1,2:T(2,128)(2,1)S(1)} %get-tuple-element.346), channel_id=1, source_target_pairs={{0,30},{2,0},{4,2},{6,4},{8,6},{10,8},{12,10},{14,12},{16,14},{18,... | collective-permute-start | bytes 11528 | tf_op jit(solution)/shard_map/while/body/eval_jaxpr/ppermute | solution.py:16
  108.9 8.2 %all-reduce.3 = bf16[2,2,9,128]{3,0,2,1:T(2,128)(2,1)S(1)} all-reduce(f32[2,2,9,128]{3,0,2,1:T(2,128)S(1)} %copy.57), channel_id=2, replica_groups=mesh['blk'=16,'band'=2] {'band'}, use_global_device_ids=true, to_apply=%region_2.2.clone | all-reduce | flops 4608 | bytes 27648 | tf_op jit(solution)/shard_map/while
  117.9 10.6 %all_to_all.17 = bf16[16,1,2,9,128]{4,2,3,1,0:T(2,128)(2,1)S(1)} all-to-all(bf16[16,1,2,9,128]{4,2,3,1,0:T(2,128)(2,1)S(1)} %get-tuple-element.195), channel_id=1, replica_groups=mesh['blk'=16,'band'=2] {'blk'}, dimensions={0} | all-to-all | bytes 147456 | tf_op jit(solution)/shard_map/all_to_all | solution.py:61
  128.5 6.5 %all_to_all.18 = bf16[16,1,2,9,128]{4,0,3,1,2:T(8,128)(2,1)S(1)} all-to-all(bf16[16,1,2,9,128]{4,0,3,1,2:T(8,128)(2,1)S(1)} %copy.41), channel_id=1, replica_groups=mesh['blk'=16,'band'=2] {'band'}, dimensions={2} | all-to-all | bytes 147456 | tf_op jit(solution)/shard_map/all_to_all | solution.py:60
  135.0 0.7 copy.43
  (164 shorter events, 24.0 us)
Async XLA Ops:
  0.0 0.8 copy-start
  0.0 0.7 copy-start.1
  11.8 0.7 copy-start.3
  13.9 0.7 copy-start.2
  14.5 3.2 %collective-permute-start = (bf16[2,3,2,160]{3,0,1,2:T(2,128)(2,1)S(1)}, bf16[2,3,2,160]{3,0,1,2:T(2,128)(2,1)S(1)}, u32[]{:S(2)}, u32[]{:S(2)}) collective-permute-start(bf16[2,3,2,160]{3,0,1,2:T(2,128)(2,1)S(1)} %get-tuple-element.346), channel_id=1, source_target_pairs={{0,30},{2,0},{4,2},{6,4},{8,6},{10,8},{12,10},{14,12},{16,14},{18,... | collective-permute-start | bytes 11528 | tf_op jit(solution)/shard_map/while/body/eval_jaxpr/ppermute | solution.py:16
  26.6 3.8 %collective-permute-start = (bf16[2,3,2,160]{3,0,1,2:T(2,128)(2,1)S(1)}, bf16[2,3,2,160]{3,0,1,2:T(2,128)(2,1)S(1)}, u32[]{:S(2)}, u32[]{:S(2)}) collective-permute-start(bf16[2,3,2,160]{3,0,1,2:T(2,128)(2,1)S(1)} %get-tuple-element.346), channel_id=1, source_target_pairs={{0,30},{2,0},{4,2},{6,4},{8,6},{10,8},{12,10},{14,12},{16,14},{18,... | collective-permute-start | bytes 11528 | tf_op jit(solution)/shard_map/while/body/eval_jaxpr/ppermute | solution.py:16
  39.9 3.8 %collective-permute-start = (bf16[2,3,2,160]{3,0,1,2:T(2,128)(2,1)S(1)}, bf16[2,3,2,160]{3,0,1,2:T(2,128)(2,1)S(1)}, u32[]{:S(2)}, u32[]{:S(2)}) collective-permute-start(bf16[2,3,2,160]{3,0,1,2:T(2,128)(2,1)S(1)} %get-tuple-element.346), channel_id=1, source_target_pairs={{0,30},{2,0},{4,2},{6,4},{8,6},{10,8},{12,10},{14,12},{16,14},{18,... | collective-permute-start | bytes 11528 | tf_op jit(solution)/shard_map/while/body/eval_jaxpr/ppermute | solution.py:16
  52.5 3.8 %collective-permute-start = (bf16[2,3,2,160]{3,0,1,2:T(2,128)(2,1)S(1)}, bf16[2,3,2,160]{3,0,1,2:T(2,128)(2,1)S(1)}, u32[]{:S(2)}, u32[]{:S(2)}) collective-permute-start(bf16[2,3,2,160]{3,0,1,2:T(2,128)(2,1)S(1)} %get-tuple-element.346), channel_id=1, source_target_pairs={{0,30},{2,0},{4,2},{6,4},{8,6},{10,8},{12,10},{14,12},{16,14},{18,... | collective-permute-start | bytes 11528 | tf_op jit(solution)/shard_map/while/body/eval_jaxpr/ppermute | solution.py:16
  65.9 3.8 %collective-permute-start = (bf16[2,3,2,160]{3,0,1,2:T(2,128)(2,1)S(1)}, bf16[2,3,2,160]{3,0,1,2:T(2,128)(2,1)S(1)}, u32[]{:S(2)}, u32[]{:S(2)}) collective-permute-start(bf16[2,3,2,160]{3,0,1,2:T(2,128)(2,1)S(1)} %get-tuple-element.346), channel_id=1, source_target_pairs={{0,30},{2,0},{4,2},{6,4},{8,6},{10,8},{12,10},{14,12},{16,14},{18,... | collective-permute-start | bytes 11528 | tf_op jit(solution)/shard_map/while/body/eval_jaxpr/ppermute | solution.py:16
  78.5 3.8 %collective-permute-start = (bf16[2,3,2,160]{3,0,1,2:T(2,128)(2,1)S(1)}, bf16[2,3,2,160]{3,0,1,2:T(2,128)(2,1)S(1)}, u32[]{:S(2)}, u32[]{:S(2)}) collective-permute-start(bf16[2,3,2,160]{3,0,1,2:T(2,128)(2,1)S(1)} %get-tuple-element.346), channel_id=1, source_target_pairs={{0,30},{2,0},{4,2},{6,4},{8,6},{10,8},{12,10},{14,12},{16,14},{18,... | collective-permute-start | bytes 11528 | tf_op jit(solution)/shard_map/while/body/eval_jaxpr/ppermute | solution.py:16
  91.9 3.8 %collective-permute-start = (bf16[2,3,2,160]{3,0,1,2:T(2,128)(2,1)S(1)}, bf16[2,3,2,160]{3,0,1,2:T(2,128)(2,1)S(1)}, u32[]{:S(2)}, u32[]{:S(2)}) collective-permute-start(bf16[2,3,2,160]{3,0,1,2:T(2,128)(2,1)S(1)} %get-tuple-element.346), channel_id=1, source_target_pairs={{0,30},{2,0},{4,2},{6,4},{8,6},{10,8},{12,10},{14,12},{16,14},{18,... | collective-permute-start | bytes 11528 | tf_op jit(solution)/shard_map/while/body/eval_jaxpr/ppermute | solution.py:16
  104.5 3.8 %collective-permute-start = (bf16[2,3,2,160]{3,0,1,2:T(2,128)(2,1)S(1)}, bf16[2,3,2,160]{3,0,1,2:T(2,128)(2,1)S(1)}, u32[]{:S(2)}, u32[]{:S(2)}) collective-permute-start(bf16[2,3,2,160]{3,0,1,2:T(2,128)(2,1)S(1)} %get-tuple-element.346), channel_id=1, source_target_pairs={{0,30},{2,0},{4,2},{6,4},{8,6},{10,8},{12,10},{14,12},{16,14},{18,... | collective-permute-start | bytes 11528 | tf_op jit(solution)/shard_map/while/body/eval_jaxpr/ppermute | solution.py:16
where the time goes:
time: 136 us
  blocking collectives  89.4 us (66%)
  starting transfers between devices  18.9 us (14%)
  local copies, waits for them, and re-layouts  11.9 us (9%)
  other arithmetic  7.15 us (5%)
  waiting for transfers between devices  5.52 us (4%)
  matrix products  2.16 us (2%)
    while x8, blocking collectives  62.4 us
    ppermute x8, starting transfers between devices, passed_along(): lax.ppermute(shard, axis, [(i, (i + by) % peers) for i in range(peers)])  18.9 us
    all_to_all x1, blocking collectives, finish(): lax.all_to_all(mirror_blocks, 'blk', split_axis=0, concat_axis=0, tiled=T...  10.6 us
    unnamed x1, blocking collectives  9.85 us
    all_to_all x1, blocking collectives, finish(): lax.all_to_all(lax.all_to_all(mirror_blocks, 'blk', split_axis=0, concat_...  6.51 us
    ppermute x8, waiting for transfers between devices, passed_along(): lax.ppermute(shard, axis, [(i, (i + by) % peers) for i in range(peers)])  5.52 us
    while x16, local copies, waits for them, and re-layouts  5.23 us
    dynamic_update_slice x8, other arithmetic, store(): own_next = lax.dynamic_update_index_in_dim(own_now, own_piece, target, 0)  5.11 us
  transfers between devices with their start and end apart: 8, of which 8 were waited for; matrix products, arithmetic and copies ran while one was open for 4% of the time, Pallas kernels for 0%

commit v1 on v0

v1 whole, which is shorter than its diff:
```python
import functools
import math

import jax
import jax.numpy as jnp
import numpy as np
from jax import lax
from jax.experimental import pallas as pl
from jax.experimental.pallas import tpu as pltpu
from jax.sharding import PartitionSpec as P

F = 320
FIRST = 15
NFFT = 1500
MAXLAG = 64
LAGS = 2 * MAXLAG
LANES = 128
COMPONENTS = 3
ROWS = 8


class Layout:
    def __init__(self, bins, bands):
        self.bins = bins
        self.bands = bands
        self.whole = bins // LANES
        self.rest = bins % LANES
        self.rest_row = 2 * COMPONENTS * self.whole
        self.chunks = 2 * self.whole + 1
        self.depth = bands * self.chunks * LANES
        assert COMPONENTS * self.rest <= LANES and 0 < 2 * self.rest <= LANES
        assert self.rest_row + 2 <= ROWS

    def column(self, band, chunk):
        return (band * self.chunks + chunk) * LANES


def lag_table(layout):
    lag_steps = 2 * np.arange(LAGS, dtype=np.int64) - 2 * MAXLAG + 1
    bins = np.arange(layout.bins * layout.bands, dtype=np.int64) + FIRST
    phases = math.pi / NFFT * ((bins[:, None] * lag_steps[None, :]) % (2 * NFFT))
    cosine = (np.cos(phases) / math.sqrt(F)).astype(np.float32)
    sine = (-np.sin(phases) / math.sqrt(F)).astype(np.float32)
    table = np.zeros((layout.depth, LAGS), np.float32)
    for band in range(layout.bands):
        first = band * layout.bins
        for chunk in range(layout.whole):
            rows = slice(first + chunk * LANES, first + (chunk + 1) * LANES)
            table[layout.column(band, 2 * chunk) :][:LANES] = cosine[rows]
            table[layout.column(band, 2 * chunk + 1) :][:LANES] = sine[rows]
        rows = slice(first + layout.whole * LANES, first + layout.bins)
        start = layout.column(band, 2 * layout.whole)
        table[start : start + layout.rest] = cosine[rows]
        table[start + layout.rest : start + 2 * layout.rest] = sine[rows]
    high = table.astype(jnp.bfloat16)
    low = (table - high.astype(np.float32)).astype(jnp.bfloat16)
    return np.concatenate([high, low], axis=1)


def pack_kernel(layout, copies, quality_ref, spectra_ref, pieces_ref, packed_ref, wide):
    stations = spectra_ref.shape[0]
    wide[...] = jnp.zeros_like(wide)
    lane = lax.broadcasted_iota(jnp.int32, (2, LANES), 1)
    for s in range(stations):
        rests = jnp.zeros((2, LANES), jnp.float32)
        for a in range(COMPONENTS):
            usable = quality_ref[s, a].astype(jnp.float32)
            both = spectra_ref[s, a].astype(jnp.float32) * usable
            for chunk in range(layout.whole):
                row = s * ROWS + 2 * (a * layout.whole + chunk)
                wide[row : row + 2, :] = both[:, chunk * LANES : (chunk + 1) * LANES]
            rest = both[:, layout.whole * LANES :]
            padded = jnp.concatenate([rest, jnp.zeros((2, LANES - layout.rest), jnp.float32)], axis=1)
            rests = rests + (pltpu.roll(padded, a * layout.rest, 1) if a else padded)
        row = s * ROWS + layout.rest_row
        wide[row : row + 2, :] = rests
    for s in range(stations):
        piece = wide[s * ROWS : (s + 1) * ROWS, :].astype(jnp.bfloat16)
        packed_ref[s] = piece
        for copy in range(copies):
            pieces_ref[copy * stations + s] = piece


def correlate_kernel(layout, peers, table_ref, pieces_ref, *rest):
    bands = layout.bands
    own_refs = rest[:bands]
    out_ref, partner, own, high, low, sums = rest[bands:]
    stations = out_ref.shape[1]
    place = lax.axis_index("band")
    partner[...] = pieces_ref[...].astype(jnp.float32).reshape(partner.shape)
    for k in range(bands):
        band = lax.rem(place + k, bands)
        start = pl.multiple_of(band * (stations * ROWS), stations * ROWS)
        own[pl.ds(start, stations * ROWS), :] = (
            own_refs[k][...].astype(jnp.float32).reshape(stations * ROWS, LANES)
        )

    lane = lax.broadcasted_iota(jnp.int32, (1, LANES), 1)
    first_half = lane < layout.rest

    def at_front(rows, component):
        shift = (LANES - component * layout.rest) % LANES
        return pltpu.roll(rows, shift, 1) if shift else rows

    def at_second(rows, component):
        shift = (LANES - (component - 1) * layout.rest) % LANES
        return pltpu.roll(rows, shift, 1) if shift else rows

    def partner_rows(band, row):
        return partner[pl.ds(band * ROWS + row, peers, stride=bands * ROWS), :]

    for band in range(bands):
        real_rest = partner_rows(band, layout.rest_row)
        imag_rest = partner_rows(band, layout.rest_row + 1)
        for b in range(COMPONENTS):
            chunks = []
            for chunk in range(layout.whole):
                row = 2 * (b * layout.whole + chunk)
                chunks.append((partner_rows(band, row), partner_rows(band, row + 1)))
            both_real = jnp.where(first_half, at_front(real_rest, b), at_second(real_rest, b))
            both_imag = jnp.where(first_half, at_front(imag_rest, b), at_second(imag_rest, b))
            for i in range(stations):
                base = (band * stations + i) * ROWS
                for a in range(COMPONENTS):
                    group = ((i * COMPONENTS + a) * COMPONENTS + b) * peers

                    def store(chunk, value):
                        column = layout.column(band, chunk)
                        upper = value.astype(jnp.bfloat16)
                        lower = value - upper.astype(jnp.float32)
                        high[group : group + peers, column : column + LANES] = upper
                        low[group : group + peers, column : column + LANES] = lower.astype(jnp.bfloat16)

                    for chunk in range(layout.whole):
                        row = base + 2 * (a * layout.whole + chunk)
                        x_real = own[row : row + 1, :]
                        x_imag = own[row + 1 : row + 2, :]
                        z_real, z_imag = chunks[chunk]
                        store(2 * chunk, x_real * z_real + x_imag * z_imag)
                        store(2 * chunk + 1, x_imag * z_real - x_real * z_imag)
                    row = base + layout.rest_row
                    x_real = own[row : row + 1, :]
                    x_imag = own[row + 1 : row + 2, :]
                    second = (lane >= layout.rest) & (lane < 2 * layout.rest)
                    zero = jnp.zeros_like(x_real)
                    with_real = jnp.where(
                        first_half, at_front(x_real, a), jnp.where(second, at_second(x_imag, a), zero)
                    )
                    with_imag = jnp.where(
                        first_half, at_front(x_imag, a), jnp.where(second, -at_second(x_real, a), zero)
                    )
                    store(2 * layout.whole, with_real * both_real + with_imag * both_imag)

    result = jnp.dot(high[...], table_ref[...], preferred_element_type=jnp.float32)
    result = (
        result[:, :LAGS]
        + result[:, LAGS:]
        + jnp.dot(low[...], table_ref[:, :LAGS], preferred_element_type=jnp.float32)
    )
    pairs = COMPONENTS * COMPONENTS
    slot = 16
    for i in range(stations):
        for ab in range(pairs):
            group = (i * pairs + ab) * peers
            sums[pl.ds(i * slot + ab, peers, stride=stations * slot), :] = result[group : group + peers]
    for v in range(peers):
        for i in range(stations):
            start = (v * stations + i) * slot
            out_ref[v, i, 0] = sums[start : start + pairs, :].astype(jnp.bfloat16)


def body(spectra, quality):
    stations = spectra.shape[0]
    peers = lax.axis_size("blk")
    bands = lax.axis_size("band")
    assert stations == bands
    layout = Layout(spectra.shape[3], bands)
    vmem = pl.BlockSpec(memory_space=pltpu.VMEM)
    pieces, packed = pl.pallas_call(
        functools.partial(pack_kernel, layout, peers),
        out_shape=(
            jax.ShapeDtypeStruct((peers * bands, ROWS, LANES), jnp.bfloat16),
            jax.ShapeDtypeStruct((stations, ROWS, LANES), jnp.bfloat16),
        ),
        in_specs=[pl.BlockSpec(memory_space=pltpu.SMEM), vmem],
        out_specs=(vmem, vmem),
        scratch_shapes=[pltpu.VMEM((stations * ROWS, LANES), jnp.float32)],
        name="pack",
    )(quality, spectra)
    own = [packed]
    for k in range(1, bands):
        own.append(lax.ppermute(packed, "band", [((i + k) % bands, i) for i in range(bands)]))
    received = lax.all_to_all(pieces, ("blk", "band"), split_axis=0, concat_axis=0, tiled=True)
    rows = stations * COMPONENTS * COMPONENTS * peers
    return pl.pallas_call(
        functools.partial(correlate_kernel, layout, peers),
        out_shape=jax.ShapeDtypeStruct(
            (peers, stations, 1, COMPONENTS * COMPONENTS, LAGS), jnp.bfloat16
        ),
        in_specs=[vmem] * (2 + bands),
        out_specs=vmem,
        scratch_shapes=[
            pltpu.VMEM((peers * bands * ROWS, LANES), jnp.float32),
            pltpu.VMEM((bands * stations * ROWS, LANES), jnp.float32),
            pltpu.VMEM((rows, layout.depth), jnp.bfloat16),
            pltpu.VMEM((rows, layout.depth), jnp.bfloat16),
            pltpu.VMEM((peers * stations * 16, LANES), jnp.float32),
        ],
        compiler_params=pltpu.CompilerParams(vmem_limit_bytes=40 * 1024 * 1024),
        name="correlate",
    )(jnp.asarray(lag_table(layout)), received, *own)


def solution(mesh):
    placed = (P("blk", None, None, "band"), P("blk", None))
    return jax.shard_map(
        body,
        mesh=mesh,
        in_specs=placed,
        out_specs=P(None, "blk", "band", None, None),
        check_vma=False,
    )
```

time: 136 us -> 18.9 us (0.14)
  blocking collectives: 89.4 us -> 0 us
  local copies, waits for them, and re-layouts: 11.9 us -> 1.69 us
  starting transfers between devices: 18.9 us -> 9.13 us
  other arithmetic: 7.15 us -> 0 us
  matrix products: 2.16 us -> 0 us
  Pallas kernels: 0 us -> 2.05 us
    while x8 -> x0, blocking collectives: 62.4 us -> none
    all_to_all x2 -> x0, blocking collectives: 17.1 us -> none  [the longest x1 10.6 us: finish(): lax.all_to_all(mirror_blocks, 'blk', split_axis=0, concat_axis=0, tiled=T...]
    ppermute x8 -> x1, starting transfers between devices: 18.9 us -> 1.83 us  [body(): lax.ppermute(packed, 'band', [((i + k) % bands, i) for i in range(bands)])]
    unnamed x1 -> x0, blocking collectives: 9.85 us -> none
    all_to_all x0 -> x1, starting transfers between devices: none -> 7.3 us  [body(): lax.all_to_all(pieces, ('blk', 'band'), split_axis=0, concat_axis=0, tile...]
    while x17 -> x0, local copies, waits for them, and re-layouts: 5.23 us -> none
    dynamic_update_slice x8 -> x0, other arithmetic: 5.11 us -> none  [store(): own_next = lax.dynamic_update_index_in_dim(own_now, own_piece, target, 0)]
    all_to_all x0 -> x1, waiting for transfers between devices: none -> 3.92 us  [body(): lax.all_to_all(pieces, ('blk', 'band'), split_axis=0, concat_axis=0, tile...]
  transfers between devices with their start and end apart: 8 -> 2, of which waited for: 8 -> 2; matrix products, arithmetic and copies ran while one was open for 4% -> 0% of each run, Pallas kernels for 0% -> 0%
where the time goes in v1:
time: 18.9 us; the launch traced here: 18.7 us
  starting transfers between devices  9.13 us (48%)
  waiting for transfers between devices  5.76 us (30%)
  Pallas kernels  2.05 us (11%)
  local copies, waits for them, and re-layouts  1.69 us (9%)
    all_to_all x1, starting transfers between devices, body(): lax.all_to_all(pieces, ('blk', 'band'), split_axis=0, concat_axis=0, tile...  7.3 us
    all_to_all x1, waiting for transfers between devices, body(): lax.all_to_all(pieces, ('blk', 'band'), split_axis=0, concat_axis=0, tile...  3.92 us
    ppermute x1, waiting for transfers between devices, body(): lax.ppermute(packed, 'band', [((i + k) % bands, i) for i in range(bands)])  1.84 us
    ppermute x1, starting transfers between devices, body(): lax.ppermute(packed, 'band', [((i + k) % bands, i) for i in range(bands)])  1.83 us
    pallas_call x1, Pallas kernels, body(): pl.pallas_call(functools.partial(pack_kernel, layout, peers), out_shape=(...  1.42 us
    unnamed x4, local copies, waits for them, and re-layouts  1 us
    pallas_call x1, local copies, waits for them, and re-layouts, body(): pl.pallas_call(functools.partial(correlate_kernel, layout, peers), out_sh...  0.69 us
    pallas_call x1, Pallas kernels, body(): pl.pallas_call(functools.partial(correlate_kernel, layout, peers), out_sh...  0.63 us
  transfers between devices with their start and end apart: 2, of which 2 were waited for; matrix products, arithmetic and copies ran while one was open for 0% of the time, Pallas kernels for 0%

profile of v1, /device:TPU:0, one launch (start us, length us, event | category | flops | bytes accessed | tf_op | source)
XLA Modules:
  0.0 18.7 jit_solution(9609916657543939903)
XLA Ops:
  0.0 1.4 %pack.1 = (bf16[32,8,128]{2,1,0:T(8,128)(2,1)}, bf16[2,8,128]{2,1,0:T(8,128)(2,1)}) custom-call(s32[2,3]{1,0:T(2,128)} %quality_ref.1, bf16[2,3,2,160]{3,2,1,0:T(2,128)(2,1)} %spectra_ref.1), custom_call_target="tpu_custom_call" | custom-call | tf_op jit(solution)/shard_map/pack/pallas_call | solution.py:179
  1.4 0.0 copy-start.1
  1.4 7.3 %all-to-all-start = ((bf16[32,8,128]{2,1,0:T(8,128)(2,1)}), bf16[32,8,128]{2,1,0:T(8,128)(2,1)S(1)}, u32[]{:S(2)}, u32[]{:S(2)}) async-start(bf16[32,8,128]{2,1,0:T(8,128)(2,1)} %get-tuple-element.7), calls=%async_computation | async-start | bytes 131072 | tf_op jit(solution)/shard_map/all_to_all | solution.py:193
  8.7 0.0 copy-done.1
  8.7 1.8 %collective-permute-start = (bf16[2,8,128]{2,1,0:T(8,128)(2,1)S(1)}, bf16[2,8,128]{2,1,0:T(8,128)(2,1)S(1)}, u32[]{:S(2)}, u32[]{:S(2)}) collective-permute-start(bf16[2,8,128]{2,1,0:T(8,128)(2,1)S(1)} %copy-done.1), channel_id=1, source_target_pairs={{1,0},{0,1},{3,2},{2,3},{5,4},{4,5},{7,6},{6,7},{9,8},{8,9},{11,10... | collective-permute-start | bytes 12296 | tf_op jit(solution)/shard_map/ppermute | solution.py:192
  10.6 1.8 %collective-permute-done.rest_1_ = bf16[2,8,128]{2,1,0:T(8,128)(2,1)S(1)} collective-permute-done((bf16[2,8,128]{2,1,0:T(8,128)(2,1)S(1)}, bf16[2,8,128]{2,1,0:T(8,128)(2,1)S(1)}, u32[]{:S(2)}, u32[]{:S(2)}) %collective-permute-start) | collective-permute-done | bytes 4128 | tf_op jit(solution)/shard_map/ppermute | solution.py:192
  12.4 3.9 %all-to-all-done.pieces_ref = bf16[32,8,128]{2,1,0:T(8,128)(2,1)S(1)} async-done(((bf16[32,8,128]{2,1,0:T(8,128)(2,1)}), bf16[32,8,128]{2,1,0:T(8,128)(2,1)S(1)}, u32[]{:S(2)}, u32[]{:S(2)}) %all-to-all-start) | async-done | bytes 65568 | tf_op jit(solution)/shard_map/all_to_all | solution.py:193
  16.3 0.0 copy-start
  16.3 1.0 %copy-done = bf16[768,256]{1,0:T(8,128)(2,1)S(1)} copy-done((bf16[768,256]{1,0:T(8,128)(2,1)S(1)}, bf16[768,256]{1,0:T(8,128)(2,1)}, u32[]{:S(2)}) %copy-start) | copy-done | bytes 393240
  17.3 0.6 %correlate.1 = bf16[16,2,1,9,128]{4,3,2,1,0:T(8,128)(2,1)S(1)} custom-call(bf16[768,256]{1,0:T(8,128)(2,1)S(1)} %copy-done, bf16[32,8,128]{2,1,0:T(8,128)(2,1)S(1)} %all-to-all-done.pieces_ref, bf16[2,8,128]{2,1,0:T(8,128)(2,1)S(1)} %copy-done.1, bf16[2,8,128]{2,1,0:T(8,128)(2,1)S(1)} %collective-permute-done.rest_1_), custom_call_target="tpu_custom_call" | custom-call | tf_op jit(solution)/shard_map/correlate/pallas_call | solution.py:195
  18.0 0.7 %copy.4 = bf16[16,2,1,9,128]{4,1,3,2,0:T(2,128)(2,1)} copy(bf16[16,2,1,9,128]{4,3,2,1,0:T(8,128)(2,1)S(1)} %correlate.1) | data formatting | bytes 147456 | tf_op jit(solution)/shard_map/correlate/pallas_call | solution.py:195
Async XLA Ops:
  1.4 7.3 %copy-start.1 = (bf16[2,8,128]{2,1,0:T(8,128)(2,1)S(1)}, bf16[2,8,128]{2,1,0:T(8,128)(2,1)}, u32[]{:S(2)}) copy-start(bf16[2,8,128]{2,1,0:T(8,128)(2,1)} %get-tuple-element.8.rest_0_) | copy-start | bytes 12292
  1.4 14.9 %all-to-all-start = ((bf16[32,8,128]{2,1,0:T(8,128)(2,1)}), bf16[32,8,128]{2,1,0:T(8,128)(2,1)S(1)}, u32[]{:S(2)}, u32[]{:S(2)}) async-start(bf16[32,8,128]{2,1,0:T(8,128)(2,1)} %get-tuple-element.7), calls=%async_computation | async-start | bytes 131072 | tf_op jit(solution)/shard_map/all_to_all | solution.py:193
  8.7 3.7 %collective-permute-start = (bf16[2,8,128]{2,1,0:T(8,128)(2,1)S(1)}, bf16[2,8,128]{2,1,0:T(8,128)(2,1)S(1)}, u32[]{:S(2)}, u32[]{:S(2)}) collective-permute-start(bf16[2,8,128]{2,1,0:T(8,128)(2,1)S(1)} %copy-done.1), channel_id=1, source_target_pairs={{1,0},{0,1},{3,2},{2,3},{5,4},{4,5},{7,6},{6,7},{9,8},{8,9},{11,10... | collective-permute-start | bytes 12296 | tf_op jit(solution)/shard_map/ppermute | solution.py:192
  16.3 1.0 %copy-start = (bf16[768,256]{1,0:T(8,128)(2,1)S(1)}, bf16[768,256]{1,0:T(8,128)(2,1)}, u32[]{:S(2)}) copy-start(bf16[768,256]{1,0:T(8,128)(2,1)} %constant.2.clone.table_ref) | copy-start | bytes 1179652

commit v2 on v1

v2 whole, which is shorter than its diff:
```python
import functools
import math

import jax
import jax.numpy as jnp
from jax import lax
from jax.experimental import pallas as pl
from jax.experimental.pallas import tpu as pltpu
from jax.sharding import PartitionSpec as P

F = 320
FIRST = 15
NFFT = 1500
MAXLAG = 64
LAGS = 2 * MAXLAG
LANES = 128
COMPONENTS = 3
PAIRS = COMPONENTS * COMPONENTS
ROWS = 8
CORES = 2
VMEM_LIMIT = 40 * 1024 * 1024


class Layout:
    def __init__(self, stations, bins, bands, peers):
        self.stations = stations
        self.bins = bins
        self.bands = bands
        self.peers = peers
        self.halves = peers // CORES
        self.slots = self.halves * bands
        self.whole = bins // LANES
        self.rest = bins % LANES
        self.rest_row = 2 * COMPONENTS * self.whole
        self.chunks = 2 * self.whole + 1
        self.depth = bands * self.chunks * LANES
        self.groups = stations * PAIRS
        self.rows = self.groups * self.halves
        assert stations == bands and stations % 2 == 0 and bins % ROWS == 0
        assert 0 < self.rest and COMPONENTS * self.rest <= LANES
        assert self.rest_row + 2 <= ROWS

    def slot(self, half, band):
        return (half * self.bands + band + 1) % self.slots

    def crossed(self, half):
        return half < self.halves // 2

    def column(self, band, chunk):
        return (band * self.chunks + chunk) * LANES


def pack_kernel(layout, quality_ref, spectra_ref, pieces_ref, wide):
    stations = layout.stations
    if layout.rest_row + 2 < ROWS:
        wide[...] = jnp.zeros_like(wide)
    for s in range(stations):
        rests = jnp.zeros((2, LANES), jnp.float32)
        for a in range(COMPONENTS):
            usable = quality_ref[s, a].astype(jnp.float32)
            both = spectra_ref[s, a].astype(jnp.float32) * usable
            for chunk in range(layout.whole):
                row = s * ROWS + 2 * (a * layout.whole + chunk)
                wide[row : row + 2, :] = both[:, chunk * LANES : (chunk + 1) * LANES]
            rest = both[:, layout.whole * LANES :]
            padded = jnp.concatenate([rest, jnp.zeros((2, LANES - layout.rest), jnp.float32)], axis=1)
            rests = rests + (pltpu.roll(padded, a * layout.rest, 1) if a else padded)
        row = s * ROWS + layout.rest_row
        wide[row : row + 2, :] = rests
    packed = [wide[s * ROWS : (s + 1) * ROWS, :] for s in range(stations)]
    for band in range(layout.bands):
        order = [packed[(band + k) % stations] for k in range(stations)]
        piece = jnp.concatenate(order).astype(jnp.bfloat16)
        for half in range(layout.halves):
            pieces_ref[layout.slot(half, band)] = piece


def at_block(layout, rows, component, block):
    shift = ((block - component) * layout.rest) % LANES
    return pltpu.roll(rows, shift, 1) if shift else rows


def lag_table(layout, anchors, table_ref):
    steps = 2 * lax.broadcasted_iota(jnp.int32, (ROWS, LAGS), 1) - 2 * MAXLAG + 1

    def wave(bins):
        index = lax.rem(bins * steps, 2 * NFFT)
        phases = math.pi / NFFT * index.astype(jnp.float32)
        return jnp.cos(phases), jnp.sin(phases)

    sublane = lax.broadcasted_iota(jnp.int32, (ROWS, LAGS), 0)
    near_cos, near_sin = wave(sublane)
    count = layout.bins * layout.bands // ROWS
    padded = -(-count // ROWS)
    for block in range(padded):
        cosine, sine = wave((sublane + block * ROWS) * ROWS + FIRST)
        anchors[0, block * ROWS : (block + 1) * ROWS, :] = cosine / math.sqrt(F)
        anchors[1, block * ROWS : (block + 1) * ROWS, :] = sine / math.sqrt(F)

    def put(start, values):
        high = values.astype(jnp.bfloat16)
        table_ref[start : start + values.shape[0], :LAGS] = high
        table_ref[start : start + values.shape[0], LAGS:] = (values - high.astype(jnp.float32)).astype(jnp.bfloat16)

    def pair(first, bins):
        cosines, sines = [], []
        for g in range(first // ROWS, (first + bins) // ROWS):
            cosine = anchors[0, g : g + 1, :]
            sine = anchors[1, g : g + 1, :]
            cosines.append(cosine * near_cos - sine * near_sin)
            sines.append(-(sine * near_cos + cosine * near_sin))
        return jnp.concatenate(cosines), jnp.concatenate(sines)

    for band in range(layout.bands):
        first = band * layout.bins
        for chunk in range(layout.whole):
            cosine, sine = pair(first + chunk * LANES, LANES)
            put(layout.column(band, 2 * chunk), cosine)
            put(layout.column(band, 2 * chunk + 1), sine)
        cosine, sine = pair(first + layout.whole * LANES, layout.rest)
        start = layout.column(band, 2 * layout.whole)
        zeros = jnp.zeros((LANES - 2 * layout.rest, LAGS), jnp.float32)
        put(start, jnp.concatenate([cosine, sine, zeros]))


def own_rows(layout, pieces_ref, own, rest_ref):
    stations = layout.stations
    here = lax.div(lax.axis_index("blk"), CORES) * layout.bands
    place = lax.axis_index("band")
    for band in range(layout.bands):
        piece = pieces_ref[lax.rem(here + band + 1, layout.slots)].astype(jnp.float32)
        for k in range(stations):
            start = pl.multiple_of((band * stations + lax.rem(place + k, stations)) * ROWS, ROWS)
            own[pl.ds(start, ROWS), :] = piece[k * ROWS : (k + 1) * ROWS]
    lane = lax.broadcasted_iota(jnp.int32, (1, LANES), 1)
    in_real = lane < layout.rest
    in_imag = (lane >= layout.rest) & (lane < 2 * layout.rest)
    zero = jnp.zeros((1, LANES), jnp.float32)
    for band in range(layout.bands):
        for i in range(stations):
            row = (band * stations + i) * ROWS + layout.rest_row
            real = own[row : row + 1, :]
            imag = own[row + 1 : row + 2, :]
            for a in range(COMPONENTS):
                to = 2 * ((band * stations + i) * COMPONENTS + a)
                rest_ref[to : to + 1, :] = jnp.where(
                    in_real, at_block(layout, real, a, 0), jnp.where(in_imag, at_block(layout, imag, a, 1), zero)
                )
                rest_ref[to + 1 : to + 2, :] = jnp.where(
                    in_real, at_block(layout, imag, a, 0), jnp.where(in_imag, -at_block(layout, real, a, 1), zero)
                )


def correlated(layout, pieces_ref, table_ref, own, rests, partner, high, low):
    for half in range(layout.halves):
        for band in range(layout.bands):
            row = (half * layout.bands + band) * ROWS
            partner[row : row + ROWS, :] = pieces_ref[layout.slot(half, band), :ROWS, :].astype(jnp.float32)

    def partner_rows(band, row):
        return partner[pl.ds(band * ROWS + row, layout.halves, stride=layout.bands * ROWS), :]

    lane = lax.broadcasted_iota(jnp.int32, (1, LANES), 1)
    in_real = lane < layout.rest
    for band in range(layout.bands):
        real_rest = partner_rows(band, layout.rest_row)
        imag_rest = partner_rows(band, layout.rest_row + 1)
        for b in range(COMPONENTS):
            first = 2 * b * layout.whole
            parts = [partner_rows(band, first + k) for k in range(2 * layout.whole)]
            both_real = jnp.where(in_real, at_block(layout, real_rest, b, 0), at_block(layout, real_rest, b, 1))
            both_imag = jnp.where(in_real, at_block(layout, imag_rest, b, 0), at_block(layout, imag_rest, b, 1))
            for a in range(COMPONENTS):
                values = [[] for _ in range(layout.chunks)]
                for i in range(layout.stations):
                    base = (band * layout.stations + i) * ROWS
                    for chunk in range(layout.whole):
                        row = base + 2 * (a * layout.whole + chunk)
                        x_real = own[row : row + 1, :]
                        x_imag = own[row + 1 : row + 2, :]
                        z_real, z_imag = parts[2 * chunk], parts[2 * chunk + 1]
                        values[2 * chunk].append(x_real * z_real + x_imag * z_imag)
                        values[2 * chunk + 1].append(x_imag * z_real - x_real * z_imag)
                    row = 2 * ((band * layout.stations + i) * COMPONENTS + a)
                    values[2 * layout.whole].append(
                        rests[row : row + 1, :] * both_real + rests[row + 1 : row + 2, :] * both_imag
                    )
                start = (b * COMPONENTS + a) * layout.stations * layout.halves
                end = start + layout.stations * layout.halves
                for chunk in range(layout.chunks):
                    value = jnp.concatenate(values[chunk])
                    upper = value.astype(jnp.bfloat16)
                    column = layout.column(band, chunk)
                    high[start:end, column : column + LANES] = upper
                    low[start:end, column : column + LANES] = (value - upper.astype(jnp.float32)).astype(jnp.bfloat16)

    both = jnp.dot(high[...], table_ref[...], preferred_element_type=jnp.float32)
    last = jnp.dot(low[...], table_ref[:, :LAGS], preferred_element_type=jnp.float32)
    return both[:, :LAGS] + (both[:, LAGS:] + last)


def near_kernel(layout, pieces_ref, sums_ref, table_ref, own_ref, rest_ref, partner, high, low, anchors):
    lag_table(layout, anchors, table_ref)
    own_rows(layout, pieces_ref, own_ref, rest_ref)
    sums_ref[...] = correlated(layout, pieces_ref, table_ref, own_ref, rest_ref, partner, high, low)


def far_kernel(layout, pieces_ref, near_ref, table_ref, own_ref, rest_ref, out_ref, partner, high, low, sums):
    far = correlated(layout, pieces_ref, table_ref, own_ref, rest_ref, partner, high, low)
    blk = lax.axis_index("blk")
    core = lax.rem(blk, CORES)
    team = jnp.where(layout.crossed(lax.div(blk, CORES)), 1 - core, core)
    halves = lax.broadcasted_iota(jnp.int32, (layout.halves, LAGS), 0)
    near_first = layout.crossed(halves).astype(jnp.int32) == team
    for b in range(COMPONENTS):
        for a in range(COMPONENTS):
            for i in range(layout.stations):
                group = (b * COMPONENTS + a) * layout.stations + i
                rows = slice(group * layout.halves, (group + 1) * layout.halves)
                for origin in range(CORES):
                    taken = near_first if origin == 0 else jnp.logical_not(near_first)
                    first = origin * layout.groups + (a * COMPONENTS + b) * layout.stations + i
                    to = pl.ds(first, layout.halves, stride=CORES * layout.groups)
                    sums[to, :] = jnp.where(taken, near_ref[rows, :], far[rows])
    out_ref[...] = sums[...].astype(jnp.bfloat16)


def body(spectra, quality):
    peers = lax.axis_size("blk")
    bands = lax.axis_size("band")
    layout = Layout(spectra.shape[0], spectra.shape[3], bands, peers)
    vmem = pl.BlockSpec(memory_space=pltpu.VMEM)
    params = pltpu.CompilerParams(vmem_limit_bytes=VMEM_LIMIT)
    piece_rows = layout.stations * ROWS
    pieces = pl.pallas_call(
        functools.partial(pack_kernel, layout),
        out_shape=pltpu.VMEM((layout.slots, piece_rows, LANES), jnp.bfloat16),
        in_specs=[pl.BlockSpec(memory_space=pltpu.SMEM), vmem],
        out_specs=vmem,
        scratch_shapes=[pltpu.VMEM((piece_rows, LANES), jnp.float32)],
        name="pack",
    )(quality, spectra)
    groups = [[0] * layout.slots for _ in range(CORES)]
    for half in range(layout.halves):
        for core in range(CORES):
            team = 1 - core if layout.crossed(half) else core
            for band in range(bands):
                groups[team][layout.slot(half, band)] = (half * CORES + core) * bands + band
    near = lax.all_to_all(
        pieces, ("blk", "band"), split_axis=0, concat_axis=0, tiled=True, axis_index_groups=groups
    )
    far = lax.ppermute(near, "blk", [(i, i ^ 1) for i in range(peers)])
    work = [
        pltpu.VMEM((layout.slots * ROWS, LANES), jnp.float32),
        pltpu.VMEM((layout.rows, layout.depth), jnp.bfloat16),
        pltpu.VMEM((layout.rows, layout.depth), jnp.bfloat16),
    ]
    kept = pl.pallas_call(
        functools.partial(near_kernel, layout),
        out_shape=(
            pltpu.VMEM((layout.rows, LAGS), jnp.float32),
            pltpu.VMEM((layout.depth, 2 * LAGS), jnp.bfloat16),
            pltpu.VMEM((bands * layout.stations * ROWS, LANES), jnp.float32),
            pltpu.VMEM((2 * bands * layout.stations * COMPONENTS, LANES), jnp.float32),
        ),
        in_specs=[vmem],
        out_specs=(vmem,) * 4,
        scratch_shapes=work
        + [pltpu.VMEM((2, -(-layout.bins * bands // (ROWS * ROWS)) * ROWS, LAGS), jnp.float32)],
        compiler_params=params,
        cost_estimate=pl.CostEstimate(flops=10**8, bytes_accessed=10**6, transcendentals=0),
        name="near",
    )(near)
    result = pl.pallas_call(
        functools.partial(far_kernel, layout),
        out_shape=jax.ShapeDtypeStruct((CORES * layout.rows, LAGS), jnp.bfloat16),
        in_specs=[vmem] * 5,
        out_specs=vmem,
        scratch_shapes=work + [pltpu.VMEM((CORES * layout.rows, LAGS), jnp.float32)],
        compiler_params=params,
        name="far",
    )(far, *kept)
    shape = (peers, 1, PAIRS, layout.stations, LAGS)
    return result.reshape(shape).transpose(0, 3, 1, 2, 4)


def solution(mesh):
    placed = (P("blk", None, None, "band"), P("blk", None))
    return jax.shard_map(
        body,
        mesh=mesh,
        in_specs=placed,
        out_specs=P(None, "blk", "band", None, None),
        check_vma=False,
    )
```

time: 18.9 us -> 15 us (0.79)
  blocking collectives: 0 us -> 11.5 us
  starting transfers between devices: 9.13 us -> 0.57 us
  waiting for transfers between devices: 5.76 us -> 0.32 us
  local copies, waits for them, and re-layouts: 1.69 us -> 0 us
  Pallas kernels: 2.05 us -> 2.36 us
    all_to_all x0 -> x1, blocking collectives: none -> 11.5 us  [body(): lax.all_to_all(pieces, ('blk', 'band'), split_axis=0, concat_axis=0, tile...]
    all_to_all x1 -> x0, starting transfers between devices: 7.3 us -> none  [body(): lax.all_to_all(pieces, ('blk', 'band'), split_axis=0, concat_axis=0, tile...]
    all_to_all x1 -> x0, waiting for transfers between devices: 3.92 us -> none  [body(): lax.all_to_all(pieces, ('blk', 'band'), split_axis=0, concat_axis=0, tile...]
    ppermute x1, waiting for transfers between devices: 1.84 us -> 0.32 us  [body(): far = lax.ppermute(near, 'blk', [(i, i ^ 1) for i in range(peers)])]
    ppermute x1, starting transfers between devices: 1.83 us -> 0.57 us  [body(): far = lax.ppermute(near, 'blk', [(i, i ^ 1) for i in range(peers)])]
    unnamed x4 -> x0, local copies, waits for them, and re-layouts: 1 us -> none
    pallas_call x1 -> x0, local copies, waits for them, and re-layouts: 0.69 us -> none  [body(): pl.pallas_call(functools.partial(correlate_kernel, layout, peers), out_sh...]
    pallas_call x2 -> x3, Pallas kernels: 2.05 us -> 2.36 us  [the longest x1 0.99 us: body(): pl.pallas_call(functools.partial(far_kernel, layout), out_shape=jax.Shape...]
  transfers between devices with their start and end apart: 2 -> 1, of which waited for: 2 -> 1; matrix products, arithmetic and copies ran while one was open for 0% -> 0% of each run, Pallas kernels for 0% -> 4%
where the time goes in v2:
time: 15 us; the launch traced here: 14.8 us
  blocking collectives  11.5 us (77%)
  Pallas kernels  2.36 us (16%)
  starting transfers between devices  0.57 us (4%)
  waiting for transfers between devices  0.32 us (2%)
    all_to_all x1, blocking collectives, body(): lax.all_to_all(pieces, ('blk', 'band'), split_axis=0, concat_axis=0, tile...  11.5 us
    pallas_call x1, Pallas kernels, body(): pl.pallas_call(functools.partial(far_kernel, layout), out_shape=jax.Shape...  0.99 us
    pallas_call x1, Pallas kernels, body(): pl.pallas_call(functools.partial(pack_kernel, layout), out_shape=pltpu.VM...  0.79 us
    pallas_call x1, Pallas kernels, body(): pl.pallas_call(functools.partial(near_kernel, layout), out_shape=(pltpu.V...  0.58 us
    ppermute x1, starting transfers between devices, body(): far = lax.ppermute(near, 'blk', [(i, i ^ 1) for i in range(peers)])  0.57 us
    ppermute x1, waiting for transfers between devices, body(): far = lax.ppermute(near, 'blk', [(i, i ^ 1) for i in range(peers)])  0.32 us
  transfers between devices with their start and end apart: 1, of which 1 were waited for; matrix products, arithmetic and copies ran while one was open for 0% of the time, Pallas kernels for 4%

profile of v2, /device:TPU:0, one launch (start us, length us, event | category | flops | bytes accessed | tf_op | source)
XLA Modules:
  0.0 14.8 jit_solution(15363031592951508140)
XLA Ops:
  0.0 0.8 %pack.1 = bf16[16,16,128]{2,1,0:T(8,128)(2,1)S(1)} custom-call(s32[2,3]{1,0:T(2,128)} %quality_ref.1, bf16[2,3,2,160]{3,2,1,0:T(2,128)(2,1)} %spectra_ref.1), custom_call_target="tpu_custom_call" | custom-call | tf_op jit(solution)/shard_map/pack/pallas_call | solution.py:235
  0.8 11.5 %all_to_all.5.pieces_ref = bf16[16,16,128]{2,1,0:T(8,128)(2,1)S(1)} all-to-all(bf16[16,16,128]{2,1,0:T(8,128)(2,1)S(1)} %pack.1), channel_id=1, replica_groups={{29,2,3,6,7,10,11,14,15,16,17,20,21,24,25,28},{31,0,1,4,5,8,9,12,13,18,..., dimensions={0} | all-to-all | bytes 131072 | tf_op jit(solution)/shard_map/all_to_all | solution.py:249
  12.3 0.6 %collective-permute-start = (bf16[16,16,128]{2,1,0:T(8,128)(2,1)S(1)}, bf16[16,16,128]{2,1,0:T(8,128)(2,1)S(1)}, u32[]{:S(2)}, u32[]{:S(2)}) collective-permute-start(bf16[16,16,128]{2,1,0:T(8,128)(2,1)S(1)} %all_to_all.5.pieces_ref), channel_id=1, source_target_pairs={{0,2},{2,0},{4,6},{6,4},{8,10},{10,8},{12,14},{14,12},{16,18},{18,... | collective-permute-start | bytes 196616 | tf_op jit(solution)/shard_map/ppermute | solution.py:252
  12.9 0.6 %near.1 = (f32[144,128]{1,0:T(8,128)S(1)}, bf16[768,256]{1,0:T(8,128)(2,1)S(1)}, f32[32,128]{1,0:T(8,128)S(1)}, f32[24,128]{1,0:T(8,128)S(1)}) custom-call(bf16[16,16,128]{2,1,0:T(8,128)(2,1)S(1)} %all_to_all.5.pieces_ref), custom_call_target="tpu_custom_call" | custom-call | flops 100000000 | bytes 1000000 | tf_op jit(solution)/shard_map/near/pallas_call | solution.py:258
  13.5 0.3 %collective-permute-done.pieces_ref = bf16[16,16,128]{2,1,0:T(8,128)(2,1)S(1)} collective-permute-done((bf16[16,16,128]{2,1,0:T(8,128)(2,1)S(1)}, bf16[16,16,128]{2,1,0:T(8,128)(2,1)S(1)}, u32[]{:S(2)}, u32[]{:S(2)}) %collective-permute-start) | collective-permute-done | bytes 65568 | tf_op jit(solution)/shard_map/ppermute | solution.py:252
  13.8 1.0 %far.1 = bf16[288,128]{1,0:T(8,128)(2,1)} custom-call(bf16[16,16,128]{2,1,0:T(8,128)(2,1)S(1)} %collective-permute-done.pieces_ref, f32[144,128]{1,0:T(8,128)S(1)} %get-tuple-element.9.near_ref, bf16[768,256]{1,0:T(8,128)(2,1)S(1)} %get-tuple-element.10.table_ref, f32[32,128]{1,0:T(8,128)S(1)} %get-tuple-element.11.own_ref, ...), custom_call_target="tpu_custom_call" | custom-call | tf_op jit(solution)/shard_map/far/pallas_call | solution.py:274
Async XLA Ops:
  12.3 1.5 %collective-permute-start = (bf16[16,16,128]{2,1,0:T(8,128)(2,1)S(1)}, bf16[16,16,128]{2,1,0:T(8,128)(2,1)S(1)}, u32[]{:S(2)}, u32[]{:S(2)}) collective-permute-start(bf16[16,16,128]{2,1,0:T(8,128)(2,1)S(1)} %all_to_all.5.pieces_ref), channel_id=1, source_target_pairs={{0,2},{2,0},{4,6},{6,4},{8,10},{10,8},{12,14},{14,12},{16,18},{18,... | collective-permute-start | bytes 196616 | tf_op jit(solution)/shard_map/ppermute | solution.py:252

commit v3 on v2

--- a/solution.py
+++ b/solution.py
@@ -155,7 +155,7 @@
     for half in range(layout.halves):
         for band in range(layout.bands):
             row = (half * layout.bands + band) * ROWS
-            partner[row : row + ROWS, :] = pieces_ref[layout.slot(half, band), :ROWS, :].astype(jnp.float32)
+            partner[row : row + ROWS, :] = pieces_ref[layout.slot(half, band)].astype(jnp.float32)[:ROWS]
 
     def partner_rows(band, row):
         return partner[pl.ds(band * ROWS + row, layout.halves, stride=layout.bands * ROWS), :]

time: 15 us -> 15 us (level)
  no operation moved by 1% of the time
where the time goes in v3:
time: 15 us; the launch traced here: 14.8 us
  blocking collectives  11.5 us (77%)
  Pallas kernels  2.36 us (16%)
  starting transfers between devices  0.57 us (4%)
  waiting for transfers between devices  0.32 us (2%)
    all_to_all x1, blocking collectives, body(): lax.all_to_all(pieces, ('blk', 'band'), split_axis=0, concat_axis=0, tile...  11.5 us
    pallas_call x1, Pallas kernels, body(): pl.pallas_call(functools.partial(far_kernel, layout), out_shape=jax.Shape...  0.99 us
    pallas_call x1, Pallas kernels, body(): pl.pallas_call(functools.partial(pack_kernel, layout), out_shape=pltpu.VM...  0.79 us
    pallas_call x1, Pallas kernels, body(): pl.pallas_call(functools.partial(near_kernel, layout), out_shape=(pltpu.V...  0.58 us
    ppermute x1, starting transfers between devices, body(): far = lax.ppermute(near, 'blk', [(i, i ^ 1) for i in range(peers)])  0.57 us
    ppermute x1, waiting for transfers between devices, body(): far = lax.ppermute(near, 'blk', [(i, i ^ 1) for i in range(peers)])  0.32 us
  transfers between devices with their start and end apart: 1, of which 1 were waited for; matrix products, arithmetic and copies ran while one was open for 0% of the time, Pallas kernels for 4%

profile of v3, /device:TPU:0, one launch (start us, length us, event | category | flops | bytes accessed | tf_op | source)
XLA Modules:
  0.0 14.8 jit_solution(15363031592951508140)
XLA Ops:
  0.0 0.8 %pack.1 = bf16[16,16,128]{2,1,0:T(8,128)(2,1)S(1)} custom-call(s32[2,3]{1,0:T(2,128)} %quality_ref.1, bf16[2,3,2,160]{3,2,1,0:T(2,128)(2,1)} %spectra_ref.1), custom_call_target="tpu_custom_call" | custom-call | tf_op jit(solution)/shard_map/pack/pallas_call | solution.py:235
  0.8 11.5 %all_to_all.5.pieces_ref = bf16[16,16,128]{2,1,0:T(8,128)(2,1)S(1)} all-to-all(bf16[16,16,128]{2,1,0:T(8,128)(2,1)S(1)} %pack.1), channel_id=1, replica_groups={{29,2,3,6,7,10,11,14,15,16,17,20,21,24,25,28},{31,0,1,4,5,8,9,12,13,18,..., dimensions={0} | all-to-all | bytes 131072 | tf_op jit(solution)/shard_map/all_to_all | solution.py:249
  12.3 0.6 %collective-permute-start = (bf16[16,16,128]{2,1,0:T(8,128)(2,1)S(1)}, bf16[16,16,128]{2,1,0:T(8,128)(2,1)S(1)}, u32[]{:S(2)}, u32[]{:S(2)}) collective-permute-start(bf16[16,16,128]{2,1,0:T(8,128)(2,1)S(1)} %all_to_all.5.pieces_ref), channel_id=1, source_target_pairs={{0,2},{2,0},{4,6},{6,4},{8,10},{10,8},{12,14},{14,12},{16,18},{18,... | collective-permute-start | bytes 196616 | tf_op jit(solution)/shard_map/ppermute | solution.py:252
  12.9 0.6 %near.1 = (f32[144,128]{1,0:T(8,128)S(1)}, bf16[768,256]{1,0:T(8,128)(2,1)S(1)}, f32[32,128]{1,0:T(8,128)S(1)}, f32[24,128]{1,0:T(8,128)S(1)}) custom-call(bf16[16,16,128]{2,1,0:T(8,128)(2,1)S(1)} %all_to_all.5.pieces_ref), custom_call_target="tpu_custom_call" | custom-call | flops 100000000 | bytes 1000000 | tf_op jit(solution)/shard_map/near/pallas_call | solution.py:258
  13.5 0.3 %collective-permute-done.pieces_ref = bf16[16,16,128]{2,1,0:T(8,128)(2,1)S(1)} collective-permute-done((bf16[16,16,128]{2,1,0:T(8,128)(2,1)S(1)}, bf16[16,16,128]{2,1,0:T(8,128)(2,1)S(1)}, u32[]{:S(2)}, u32[]{:S(2)}) %collective-permute-start) | collective-permute-done | bytes 65568 | tf_op jit(solution)/shard_map/ppermute | solution.py:252
  13.8 1.0 %far.1 = bf16[288,128]{1,0:T(8,128)(2,1)} custom-call(bf16[16,16,128]{2,1,0:T(8,128)(2,1)S(1)} %collective-permute-done.pieces_ref, f32[144,128]{1,0:T(8,128)S(1)} %get-tuple-element.9.near_ref, bf16[768,256]{1,0:T(8,128)(2,1)S(1)} %get-tuple-element.10.table_ref, f32[32,128]{1,0:T(8,128)S(1)} %get-tuple-element.11.own_ref, ...), custom_call_target="tpu_custom_call" | custom-call | tf_op jit(solution)/shard_map/far/pallas_call | solution.py:274
Async XLA Ops:
  12.3 1.5 %collective-permute-start = (bf16[16,16,128]{2,1,0:T(8,128)(2,1)S(1)}, bf16[16,16,128]{2,1,0:T(8,128)(2,1)S(1)}, u32[]{:S(2)}, u32[]{:S(2)}) collective-permute-start(bf16[16,16,128]{2,1,0:T(8,128)(2,1)S(1)} %all_to_all.5.pieces_ref), channel_id=1, source_target_pairs={{0,2},{2,0},{4,6},{6,4},{8,10},{10,8},{12,14},{14,12},{16,18},{18,... | collective-permute-start | bytes 196616 | tf_op jit(solution)/shard_map/ppermute | solution.py:252

commit v4 on v3

--- a/solution.py
+++ b/solution.py
@@ -151,7 +151,7 @@
                 )
 
 
-def correlated(layout, pieces_ref, table_ref, own, rests, partner, high, low):
+def correlated(layout, pieces_ref, table_ref, own, rests, partner):
     for half in range(layout.halves):
         for band in range(layout.bands):
             row = (half * layout.bands + band) * ROWS
@@ -162,16 +162,17 @@
 
     lane = lax.broadcasted_iota(jnp.int32, (1, LANES), 1)
     in_real = lane < layout.rest
+    uppers, lowers = [], []
     for band in range(layout.bands):
         real_rest = partner_rows(band, layout.rest_row)
         imag_rest = partner_rows(band, layout.rest_row + 1)
+        columns = [[] for _ in range(layout.chunks)]
         for b in range(COMPONENTS):
             first = 2 * b * layout.whole
             parts = [partner_rows(band, first + k) for k in range(2 * layout.whole)]
             both_real = jnp.where(in_real, at_block(layout, real_rest, b, 0), at_block(layout, real_rest, b, 1))
             both_imag = jnp.where(in_real, at_block(layout, imag_rest, b, 0), at_block(layout, imag_rest, b, 1))
             for a in range(COMPONENTS):
-                values = [[] for _ in range(layout.chunks)]
                 for i in range(layout.stations):
                     base = (band * layout.stations + i) * ROWS
                     for chunk in range(layout.whole):
@@ -179,34 +180,30 @@
                         x_real = own[row : row + 1, :]
                         x_imag = own[row + 1 : row + 2, :]
                         z_real, z_imag = parts[2 * chunk], parts[2 * chunk + 1]
-                        values[2 * chunk].append(x_real * z_real + x_imag * z_imag)
-                        values[2 * chunk + 1].append(x_imag * z_real - x_real * z_imag)
+                        columns[2 * chunk].append(x_real * z_real + x_imag * z_imag)
+                        columns[2 * chunk + 1].append(x_imag * z_real - x_real * z_imag)
                     row = 2 * ((band * layout.stations + i) * COMPONENTS + a)
-                    values[2 * layout.whole].append(
+                    columns[2 * layout.whole].append(
                         rests[row : row + 1, :] * both_real + rests[row + 1 : row + 2, :] * both_imag
                     )
-                start = (b * COMPONENTS + a) * layout.stations * layout.halves
-                end = start + layout.stations * layout.halves
-                for chunk in range(layout.chunks):
-                    value = jnp.concatenate(values[chunk])
-                    upper = value.astype(jnp.bfloat16)
-                    column = layout.column(band, chunk)
-                    high[start:end, column : column + LANES] = upper
-                    low[start:end, column : column + LANES] = (value - upper.astype(jnp.float32)).astype(jnp.bfloat16)
-
-    both = jnp.dot(high[...], table_ref[...], preferred_element_type=jnp.float32)
-    last = jnp.dot(low[...], table_ref[:, :LAGS], preferred_element_type=jnp.float32)
+        values = jnp.concatenate([jnp.concatenate(column) for column in columns], axis=1)
+        upper = values.astype(jnp.bfloat16)
+        lower = (values - upper.astype(jnp.float32)).astype(jnp.bfloat16)
+        uppers.append(upper)
+        lowers.append(lower)
+    both = jnp.dot(jnp.concatenate(uppers, axis=1), table_ref[...], preferred_element_type=jnp.float32)
+    last = jnp.dot(jnp.concatenate(lowers, axis=1), table_ref[:, :LAGS], preferred_element_type=jnp.float32)
     return both[:, :LAGS] + (both[:, LAGS:] + last)
 
 
-def near_kernel(layout, pieces_ref, sums_ref, table_ref, own_ref, rest_ref, partner, high, low, anchors):
+def near_kernel(layout, pieces_ref, sums_ref, table_ref, own_ref, rest_ref, partner, anchors):
     lag_table(layout, anchors, table_ref)
     own_rows(layout, pieces_ref, own_ref, rest_ref)
-    sums_ref[...] = correlated(layout, pieces_ref, table_ref, own_ref, rest_ref, partner, high, low)
-
-
-def far_kernel(layout, pieces_ref, near_ref, table_ref, own_ref, rest_ref, out_ref, partner, high, low, sums):
-    far = correlated(layout, pieces_ref, table_ref, own_ref, rest_ref, partner, high, low)
+    sums_ref[...] = correlated(layout, pieces_ref, table_ref, own_ref, rest_ref, partner)
+
+
+def far_kernel(layout, pieces_ref, near_ref, table_ref, own_ref, rest_ref, out_ref, partner, sums):
+    far = correlated(layout, pieces_ref, table_ref, own_ref, rest_ref, partner)
     blk = lax.axis_index("blk")
     core = lax.rem(blk, CORES)
     team = jnp.where(layout.crossed(lax.div(blk, CORES)), 1 - core, core)
@@ -250,11 +247,7 @@
         pieces, ("blk", "band"), split_axis=0, concat_axis=0, tiled=True, axis_index_groups=groups
     )
     far = lax.ppermute(near, "blk", [(i, i ^ 1) for i in range(peers)])
-    work = [
-        pltpu.VMEM((layout.slots * ROWS, LANES), jnp.float32),
-        pltpu.VMEM((layout.rows, layout.depth), jnp.bfloat16),
-        pltpu.VMEM((layout.rows, layout.depth), jnp.bfloat16),
-    ]
+    partner = pltpu.VMEM((layout.slots * ROWS, LANES), jnp.float32)
     kept = pl.pallas_call(
         functools.partial(near_kernel, layout),
         out_shape=(
@@ -265,8 +258,10 @@
         ),
         in_specs=[vmem],
         out_specs=(vmem,) * 4,
-        scratch_shapes=work
-        + [pltpu.VMEM((2, -(-layout.bins * bands // (ROWS * ROWS)) * ROWS, LAGS), jnp.float32)],
+        scratch_shapes=[
+            partner,
+            pltpu.VMEM((2, -(-layout.bins * bands // (ROWS * ROWS)) * ROWS, LAGS), jnp.float32),
+        ],
         compiler_params=params,
         cost_estimate=pl.CostEstimate(flops=10**8, bytes_accessed=10**6, transcendentals=0),
         name="near",
@@ -276,7 +271,7 @@
         out_shape=jax.ShapeDtypeStruct((CORES * layout.rows, LAGS), jnp.bfloat16),
         in_specs=[vmem] * 5,
         out_specs=vmem,
-        scratch_shapes=work + [pltpu.VMEM((CORES * layout.rows, LAGS), jnp.float32)],
+        scratch_shapes=[partner, pltpu.VMEM((CORES * layout.rows, LAGS), jnp.float32)],
         compiler_params=params,
         name="far",
     )(far, *kept)

time: 15 us -> 15 us (level)
  no operation moved by 1% of the time
where the time goes in v4:
time: 15 us; the launch traced here: 14.7 us
  blocking collectives  11.5 us (77%)
  Pallas kernels  2.27 us (15%)
  starting transfers between devices  0.57 us (4%)
  waiting for transfers between devices  0.38 us (3%)
    all_to_all x1, blocking collectives, body(): lax.all_to_all(pieces, ('blk', 'band'), split_axis=0, concat_axis=0, tile...  11.5 us
    pallas_call x1, Pallas kernels, body(): pl.pallas_call(functools.partial(far_kernel, layout), out_shape=jax.Shape...  0.96 us
    pallas_call x1, Pallas kernels, body(): pl.pallas_call(functools.partial(pack_kernel, layout), out_shape=pltpu.VM...  0.79 us
    ppermute x1, starting transfers between devices, body(): far = lax.ppermute(near, 'blk', [(i, i ^ 1) for i in range(peers)])  0.57 us
    pallas_call x1, Pallas kernels, body(): pl.pallas_call(functools.partial(near_kernel, layout), out_shape=(pltpu.V...  0.52 us
    ppermute x1, waiting for transfers between devices, body(): far = lax.ppermute(near, 'blk', [(i, i ^ 1) for i in range(peers)])  0.38 us
  transfers between devices with their start and end apart: 1, of which 1 were waited for; matrix products, arithmetic and copies ran while one was open for 0% of the time, Pallas kernels for 4%

profile of v4, /device:TPU:0, one launch (start us, length us, event | category | flops | bytes accessed | tf_op | source)
XLA Modules:
  0.0 14.7 jit_solution(1937194312591535126)
XLA Ops:
  0.0 0.8 %pack.1 = bf16[16,16,128]{2,1,0:T(8,128)(2,1)S(1)} custom-call(s32[2,3]{1,0:T(2,128)} %quality_ref.1, bf16[2,3,2,160]{3,2,1,0:T(2,128)(2,1)} %spectra_ref.1), custom_call_target="tpu_custom_call" | custom-call | tf_op jit(solution)/shard_map/pack/pallas_call | solution.py:232
  0.8 11.5 %all_to_all.5.pieces_ref = bf16[16,16,128]{2,1,0:T(8,128)(2,1)S(1)} all-to-all(bf16[16,16,128]{2,1,0:T(8,128)(2,1)S(1)} %pack.1), channel_id=1, replica_groups={{29,2,3,6,7,10,11,14,15,16,17,20,21,24,25,28},{31,0,1,4,5,8,9,12,13,18,..., dimensions={0} | all-to-all | bytes 131072 | tf_op jit(solution)/shard_map/all_to_all | solution.py:246
  12.3 0.6 %collective-permute-start = (bf16[16,16,128]{2,1,0:T(8,128)(2,1)S(1)}, bf16[16,16,128]{2,1,0:T(8,128)(2,1)S(1)}, u32[]{:S(2)}, u32[]{:S(2)}) collective-permute-start(bf16[16,16,128]{2,1,0:T(8,128)(2,1)S(1)} %all_to_all.5.pieces_ref), channel_id=1, source_target_pairs={{0,2},{2,0},{4,6},{6,4},{8,10},{10,8},{12,14},{14,12},{16,18},{18,... | collective-permute-start | bytes 196616 | tf_op jit(solution)/shard_map/ppermute | solution.py:249
  12.9 0.5 %near.1 = (f32[144,128]{1,0:T(8,128)S(1)}, bf16[768,256]{1,0:T(8,128)(2,1)S(1)}, f32[32,128]{1,0:T(8,128)S(1)}, f32[24,128]{1,0:T(8,128)S(1)}) custom-call(bf16[16,16,128]{2,1,0:T(8,128)(2,1)S(1)} %all_to_all.5.pieces_ref), custom_call_target="tpu_custom_call" | custom-call | flops 100000000 | bytes 1000000 | tf_op jit(solution)/shard_map/near/pallas_call | solution.py:251
  13.4 0.4 %collective-permute-done.pieces_ref = bf16[16,16,128]{2,1,0:T(8,128)(2,1)S(1)} collective-permute-done((bf16[16,16,128]{2,1,0:T(8,128)(2,1)S(1)}, bf16[16,16,128]{2,1,0:T(8,128)(2,1)S(1)}, u32[]{:S(2)}, u32[]{:S(2)}) %collective-permute-start) | collective-permute-done | bytes 65568 | tf_op jit(solution)/shard_map/ppermute | solution.py:249
  13.8 1.0 %far.1 = bf16[288,128]{1,0:T(8,128)(2,1)} custom-call(bf16[16,16,128]{2,1,0:T(8,128)(2,1)S(1)} %collective-permute-done.pieces_ref, f32[144,128]{1,0:T(8,128)S(1)} %get-tuple-element.9.near_ref, bf16[768,256]{1,0:T(8,128)(2,1)S(1)} %get-tuple-element.10.table_ref, f32[32,128]{1,0:T(8,128)S(1)} %get-tuple-element.11.own_ref, ...), custom_call_target="tpu_custom_call" | custom-call | tf_op jit(solution)/shard_map/far/pallas_call | solution.py:269
Async XLA Ops:
  12.3 1.5 %collective-permute-start = (bf16[16,16,128]{2,1,0:T(8,128)(2,1)S(1)}, bf16[16,16,128]{2,1,0:T(8,128)(2,1)S(1)}, u32[]{:S(2)}, u32[]{:S(2)}) collective-permute-start(bf16[16,16,128]{2,1,0:T(8,128)(2,1)S(1)} %all_to_all.5.pieces_ref), channel_id=1, source_target_pairs={{0,2},{2,0},{4,6},{6,4},{8,10},{10,8},{12,14},{14,12},{16,18},{18,... | collective-permute-start | bytes 196616 | tf_op jit(solution)/shard_map/ppermute | solution.py:249

commit v5 on v4

--- a/solution.py
+++ b/solution.py
@@ -47,7 +47,9 @@
         return half < self.halves // 2
 
     def column(self, band, chunk):
-        return (band * self.chunks + chunk) * LANES
+        whole = self.chunks - 1
+        place = band * whole + chunk if chunk < whole else self.bands * whole + band
+        return place * LANES
 
 
 def pack_kernel(layout, quality_ref, spectra_ref, pieces_ref, wide):
@@ -162,7 +164,7 @@
 
     lane = lax.broadcasted_iota(jnp.int32, (1, LANES), 1)
     in_real = lane < layout.rest
-    uppers, lowers = [], []
+    values = {}
     for band in range(layout.bands):
         real_rest = partner_rows(band, layout.rest_row)
         imag_rest = partner_rows(band, layout.rest_row + 1)
@@ -186,11 +188,11 @@
                     columns[2 * layout.whole].append(
                         rests[row : row + 1, :] * both_real + rests[row + 1 : row + 2, :] * both_imag
                     )
-        values = jnp.concatenate([jnp.concatenate(column) for column in columns], axis=1)
-        upper = values.astype(jnp.bfloat16)
-        lower = (values - upper.astype(jnp.float32)).astype(jnp.bfloat16)
-        uppers.append(upper)
-        lowers.append(lower)
+        for chunk in range(layout.chunks):
+            values[layout.column(band, chunk)] = jnp.concatenate(columns[chunk])
+    values = [values[column] for column in sorted(values)]
+    uppers = [value.astype(jnp.bfloat16) for value in values]
+    lowers = [(value - upper.astype(jnp.float32)).astype(jnp.bfloat16) for value, upper in zip(values, uppers)]
     both = jnp.dot(jnp.concatenate(uppers, axis=1), table_ref[...], preferred_element_type=jnp.float32)
     last = jnp.dot(jnp.concatenate(lowers, axis=1), table_ref[:, :LAGS], preferred_element_type=jnp.float32)
     return both[:, :LAGS] + (both[:, LAGS:] + last)
@@ -246,7 +248,7 @@
     near = lax.all_to_all(
         pieces, ("blk", "band"), split_axis=0, concat_axis=0, tiled=True, axis_index_groups=groups
     )
-    far = lax.ppermute(near, "blk", [(i, i ^ 1) for i in range(peers)])
+    far = lax.ppermute(near[:, :ROWS], "blk", [(i, i ^ 1) for i in range(peers)])
     partner = pltpu.VMEM((layout.slots * ROWS, LANES), jnp.float32)
     kept = pl.pallas_call(
         functools.partial(near_kernel, layout),

time: 15 us -> 14.9 us (level)
  no operation moved by 1% of the time
where the time goes in v5:
time: 14.9 us; the launch traced here: 14.7 us
  blocking collectives  11.5 us (77%)
  Pallas kernels  2.26 us (15%)
  starting transfers between devices  0.57 us (4%)
  waiting for transfers between devices  0.33 us (2%)
    all_to_all x1, blocking collectives, body(): lax.all_to_all(pieces, ('blk', 'band'), split_axis=0, concat_axis=0, tile...  11.5 us
    pallas_call x1, Pallas kernels, body(): pl.pallas_call(functools.partial(far_kernel, layout), out_shape=jax.Shape...  0.95 us
    pallas_call x1, Pallas kernels, body(): pl.pallas_call(functools.partial(pack_kernel, layout), out_shape=pltpu.VM...  0.79 us
    ppermute x1, starting transfers between devices, body(): lax.ppermute(near[:, :ROWS], 'blk', [(i, i ^ 1) for i in range(peers)])  0.57 us
    pallas_call x1, Pallas kernels, body(): pl.pallas_call(functools.partial(near_kernel, layout), out_shape=(pltpu.V...  0.52 us
    ppermute x1, waiting for transfers between devices, body(): lax.ppermute(near[:, :ROWS], 'blk', [(i, i ^ 1) for i in range(peers)])  0.33 us
  transfers between devices with their start and end apart: 1, of which 1 were waited for; matrix products, arithmetic and copies ran while one was open for 0% of the time, Pallas kernels for 4%

profile of v5, /device:TPU:0, one launch (start us, length us, event | category | flops | bytes accessed | tf_op | source)
XLA Modules:
  0.0 14.7 jit_solution(16926733624482840551)
XLA Ops:
  0.0 0.8 %pack.1 = bf16[16,16,128]{2,1,0:T(8,128)(2,1)S(1)} custom-call(s32[2,3]{1,0:T(2,128)} %quality_ref.1, bf16[2,3,2,160]{3,2,1,0:T(2,128)(2,1)} %spectra_ref.1), custom_call_target="tpu_custom_call" | custom-call | tf_op jit(solution)/shard_map/pack/pallas_call | solution.py:234
  0.8 11.5 %all_to_all.5.pieces_ref = bf16[16,16,128]{2,1,0:T(8,128)(2,1)S(1)} all-to-all(bf16[16,16,128]{2,1,0:T(8,128)(2,1)S(1)} %pack.1), channel_id=1, replica_groups={{29,2,3,6,7,10,11,14,15,16,17,20,21,24,25,28},{31,0,1,4,5,8,9,12,13,18,..., dimensions={0} | all-to-all | bytes 131072 | tf_op jit(solution)/shard_map/all_to_all | solution.py:248
  12.3 0.6 %collective-permute-start = (bf16[16,8,128]{2,1,0:T(8,128)(2,1)S(1)}, bf16[16,8,128]{2,1,0:T(8,128)(2,1)S(1)}, u32[]{:S(2)}, u32[]{:S(2)}) collective-permute-start(bf16[16,8,128]{2,1,0:T(8,128)(2,1)S(1)} %slice.4), channel_id=1, source_target_pairs={{0,2},{2,0},{4,6},{6,4},{8,10},{10,8},{12,14},{14,12},{16,18},{18,... | collective-permute-start | bytes 98312 | tf_op jit(solution)/shard_map/ppermute | solution.py:251
  12.9 0.5 %near.1 = (f32[144,128]{1,0:T(8,128)S(1)}, bf16[768,256]{1,0:T(8,128)(2,1)S(1)}, f32[32,128]{1,0:T(8,128)S(1)}, f32[24,128]{1,0:T(8,128)S(1)}) custom-call(bf16[16,16,128]{2,1,0:T(8,128)(2,1)S(1)} %all_to_all.5.pieces_ref), custom_call_target="tpu_custom_call" | custom-call | flops 100000000 | bytes 1000000 | tf_op jit(solution)/shard_map/near/pallas_call | solution.py:253
  13.4 0.3 %collective-permute-done.pieces_ref = bf16[16,8,128]{2,1,0:T(8,128)(2,1)S(1)} collective-permute-done((bf16[16,8,128]{2,1,0:T(8,128)(2,1)S(1)}, bf16[16,8,128]{2,1,0:T(8,128)(2,1)S(1)}, u32[]{:S(2)}, u32[]{:S(2)}) %collective-permute-start) | collective-permute-done | bytes 32800 | tf_op jit(solution)/shard_map/ppermute | solution.py:251
  13.7 0.9 %far.1 = bf16[288,128]{1,0:T(8,128)(2,1)} custom-call(bf16[16,8,128]{2,1,0:T(8,128)(2,1)S(1)} %collective-permute-done.pieces_ref, f32[144,128]{1,0:T(8,128)S(1)} %get-tuple-element.9.near_ref, bf16[768,256]{1,0:T(8,128)(2,1)S(1)} %get-tuple-element.10.table_ref, f32[32,128]{1,0:T(8,128)S(1)} %get-tuple-element.11.own_ref, ...), custom_call_target="tpu_custom_call" | custom-call | tf_op jit(solution)/shard_map/far/pallas_call | solution.py:271
  (1 shorter events, 0.0 us)
Async XLA Ops:
  12.3 1.4 %collective-permute-start = (bf16[16,8,128]{2,1,0:T(8,128)(2,1)S(1)}, bf16[16,8,128]{2,1,0:T(8,128)(2,1)S(1)}, u32[]{:S(2)}, u32[]{:S(2)}) collective-permute-start(bf16[16,8,128]{2,1,0:T(8,128)(2,1)S(1)} %slice.4), channel_id=1, source_target_pairs={{0,2},{2,0},{4,6},{6,4},{8,10},{10,8},{12,14},{14,12},{16,18},{18,... | collective-permute-start | bytes 98312 | tf_op jit(solution)/shard_map/ppermute | solution.py:251

commit v6 on v5

--- a/solution.py
+++ b/solution.py
@@ -32,24 +32,27 @@
         self.whole = bins // LANES
         self.rest = bins % LANES
         self.rest_row = 2 * COMPONENTS * self.whole
-        self.chunks = 2 * self.whole + 1
-        self.depth = bands * self.chunks * LANES
+        self.main = bands * 2 * self.whole
+        self.per = LANES // (2 * self.rest)
+        self.tails = -(-bands // self.per)
+        self.depth = (self.main + self.tails) * LANES
         self.groups = stations * PAIRS
         self.rows = self.groups * self.halves
         assert stations == bands and stations % 2 == 0 and bins % ROWS == 0
         assert 0 < self.rest and COMPONENTS * self.rest <= LANES
         assert self.rest_row + 2 <= ROWS
 
+    def row(self, component, chunk):
+        return 2 * (component * self.whole + chunk)
+
     def slot(self, half, band):
         return (half * self.bands + band + 1) % self.slots
 
     def crossed(self, half):
         return half < self.halves // 2
 
-    def column(self, band, chunk):
-        whole = self.chunks - 1
-        place = band * whole + chunk if chunk < whole else self.bands * whole + band
-        return place * LANES
+    def bands_of(self, tail):
+        return range(tail * self.per, min((tail + 1) * self.per, self.bands))
 
 
 def pack_kernel(layout, quality_ref, spectra_ref, pieces_ref, wide):
@@ -99,10 +102,13 @@
         anchors[0, block * ROWS : (block + 1) * ROWS, :] = cosine / math.sqrt(F)
         anchors[1, block * ROWS : (block + 1) * ROWS, :] = sine / math.sqrt(F)
 
-    def put(start, values):
+    def put(chunk, values):
         high = values.astype(jnp.bfloat16)
-        table_ref[start : start + values.shape[0], :LAGS] = high
-        table_ref[start : start + values.shape[0], LAGS:] = (values - high.astype(jnp.float32)).astype(jnp.bfloat16)
+        low = (values - high.astype(jnp.float32)).astype(jnp.bfloat16)
+        many, place = (layout.main, chunk) if chunk < layout.main else (layout.tails, layout.main + chunk)
+        for start in (place * LANES, (place + many) * LANES):
+            table_ref[start : start + LANES, :LAGS] = high
+            table_ref[start : start + LANES, LAGS:] = low
 
     def pair(first, bins):
         cosines, sines = [], []
@@ -114,15 +120,18 @@
         return jnp.concatenate(cosines), jnp.concatenate(sines)
 
     for band in range(layout.bands):
-        first = band * layout.bins
         for chunk in range(layout.whole):
-            cosine, sine = pair(first + chunk * LANES, LANES)
-            put(layout.column(band, 2 * chunk), cosine)
-            put(layout.column(band, 2 * chunk + 1), sine)
-        cosine, sine = pair(first + layout.whole * LANES, layout.rest)
-        start = layout.column(band, 2 * layout.whole)
-        zeros = jnp.zeros((LANES - 2 * layout.rest, LAGS), jnp.float32)
-        put(start, jnp.concatenate([cosine, sine, zeros]))
+            cosine, sine = pair(band * layout.bins + chunk * LANES, LANES)
+            put(2 * (band * layout.whole + chunk), cosine)
+            put(2 * (band * layout.whole + chunk) + 1, sine)
+    for tail in range(layout.tails):
+        parts = []
+        for band in layout.bands_of(tail):
+            parts.extend(pair(band * layout.bins + layout.whole * LANES, layout.rest))
+        spare = LANES - len(parts) * layout.rest
+        if spare:
+            parts.append(jnp.zeros((spare, LAGS), jnp.float32))
+        put(layout.main + tail, jnp.concatenate(parts))
 
 
 def own_rows(layout, pieces_ref, own, rest_ref):
@@ -134,23 +143,23 @@
         for k in range(stations):
             start = pl.multiple_of((band * stations + lax.rem(place + k, stations)) * ROWS, ROWS)
             own[pl.ds(start, ROWS), :] = piece[k * ROWS : (k + 1) * ROWS]
-    lane = lax.broadcasted_iota(jnp.int32, (1, LANES), 1)
-    in_real = lane < layout.rest
-    in_imag = (lane >= layout.rest) & (lane < 2 * layout.rest)
-    zero = jnp.zeros((1, LANES), jnp.float32)
-    for band in range(layout.bands):
+    block = lax.div(lax.broadcasted_iota(jnp.int32, (1, LANES), 1), layout.rest)
+    for tail in range(layout.tails):
         for i in range(stations):
-            row = (band * stations + i) * ROWS + layout.rest_row
-            real = own[row : row + 1, :]
-            imag = own[row + 1 : row + 2, :]
             for a in range(COMPONENTS):
-                to = 2 * ((band * stations + i) * COMPONENTS + a)
-                rest_ref[to : to + 1, :] = jnp.where(
-                    in_real, at_block(layout, real, a, 0), jnp.where(in_imag, at_block(layout, imag, a, 1), zero)
-                )
-                rest_ref[to + 1 : to + 2, :] = jnp.where(
-                    in_real, at_block(layout, imag, a, 0), jnp.where(in_imag, -at_block(layout, real, a, 1), zero)
-                )
+                with_real = with_imag = jnp.zeros((1, LANES), jnp.float32)
+                for k, band in enumerate(layout.bands_of(tail)):
+                    row = (band * stations + i) * ROWS + layout.rest_row
+                    real = own[row : row + 1, :]
+                    imag = own[row + 1 : row + 2, :]
+                    first, second = block == 2 * k, block == 2 * k + 1
+                    with_real = jnp.where(first, at_block(layout, real, a, 2 * k), with_real)
+                    with_real = jnp.where(second, at_block(layout, imag, a, 2 * k + 1), with_real)
+                    with_imag = jnp.where(first, at_block(layout, imag, a, 2 * k), with_imag)
+                    with_imag = jnp.where(second, -at_block(layout, real, a, 2 * k + 1), with_imag)
+                to = 2 * ((tail * stations + i) * COMPONENTS + a)
+                rest_ref[to : to + 1, :] = with_real
+                rest_ref[to + 1 : to + 2, :] = with_imag
 
 
 def correlated(layout, pieces_ref, table_ref, own, rests, partner):
@@ -162,40 +171,48 @@
     def partner_rows(band, row):
         return partner[pl.ds(band * ROWS + row, layout.halves, stride=layout.bands * ROWS), :]
 
-    lane = lax.broadcasted_iota(jnp.int32, (1, LANES), 1)
-    in_real = lane < layout.rest
-    values = {}
+    values = []
     for band in range(layout.bands):
-        real_rest = partner_rows(band, layout.rest_row)
-        imag_rest = partner_rows(band, layout.rest_row + 1)
-        columns = [[] for _ in range(layout.chunks)]
+        for chunk in range(layout.whole):
+            reals, imags = [], []
+            for b in range(COMPONENTS):
+                z_real = partner_rows(band, layout.row(b, chunk))
+                z_imag = partner_rows(band, layout.row(b, chunk) + 1)
+                for a in range(COMPONENTS):
+                    for i in range(layout.stations):
+                        row = (band * layout.stations + i) * ROWS + layout.row(a, chunk)
+                        x_real = own[row : row + 1, :]
+                        x_imag = own[row + 1 : row + 2, :]
+                        reals.append(x_real * z_real + x_imag * z_imag)
+                        imags.append(x_imag * z_real - x_real * z_imag)
+            values.append(jnp.concatenate(reals))
+            values.append(jnp.concatenate(imags))
+    block = lax.div(lax.broadcasted_iota(jnp.int32, (1, LANES), 1), layout.rest)
+    for tail in range(layout.tails):
+        rows = [
+            (partner_rows(band, layout.rest_row), partner_rows(band, layout.rest_row + 1))
+            for band in layout.bands_of(tail)
+        ]
+        parts = []
         for b in range(COMPONENTS):
-            first = 2 * b * layout.whole
-            parts = [partner_rows(band, first + k) for k in range(2 * layout.whole)]
-            both_real = jnp.where(in_real, at_block(layout, real_rest, b, 0), at_block(layout, real_rest, b, 1))
-            both_imag = jnp.where(in_real, at_block(layout, imag_rest, b, 0), at_block(layout, imag_rest, b, 1))
+            z_real = z_imag = None
+            for k, (real, imag) in enumerate(rows):
+                for place in (2 * k, 2 * k + 1):
+                    turned_real = at_block(layout, real, b, place)
+                    turned_imag = at_block(layout, imag, b, place)
+                    z_real = turned_real if z_real is None else jnp.where(block >= place, turned_real, z_real)
+                    z_imag = turned_imag if z_imag is None else jnp.where(block >= place, turned_imag, z_imag)
             for a in range(COMPONENTS):
                 for i in range(layout.stations):
-                    base = (band * layout.stations + i) * ROWS
-                    for chunk in range(layout.whole):
-                        row = base + 2 * (a * layout.whole + chunk)
-                        x_real = own[row : row + 1, :]
-                        x_imag = own[row + 1 : row + 2, :]
-                        z_real, z_imag = parts[2 * chunk], parts[2 * chunk + 1]
-                        columns[2 * chunk].append(x_real * z_real + x_imag * z_imag)
-                        columns[2 * chunk + 1].append(x_imag * z_real - x_real * z_imag)
-                    row = 2 * ((band * layout.stations + i) * COMPONENTS + a)
-                    columns[2 * layout.whole].append(
-                        rests[row : row + 1, :] * both_real + rests[row + 1 : row + 2, :] * both_imag
-                    )
-        for chunk in range(layout.chunks):
-            values[layout.column(band, chunk)] = jnp.concatenate(columns[chunk])
-    values = [values[column] for column in sorted(values)]
-    uppers = [value.astype(jnp.bfloat16) for value in values]
-    lowers = [(value - upper.astype(jnp.float32)).astype(jnp.bfloat16) for value, upper in zip(values, uppers)]
-    both = jnp.dot(jnp.concatenate(uppers, axis=1), table_ref[...], preferred_element_type=jnp.float32)
-    last = jnp.dot(jnp.concatenate(lowers, axis=1), table_ref[:, :LAGS], preferred_element_type=jnp.float32)
-    return both[:, :LAGS] + (both[:, LAGS:] + last)
+                    row = 2 * ((tail * layout.stations + i) * COMPONENTS + a)
+                    parts.append(rests[row : row + 1, :] * z_real + rests[row + 1 : row + 2, :] * z_imag)
+        values.append(jnp.concatenate(parts))
+    highs = [value.astype(jnp.bfloat16) for value in values]
+    lows = [(value - high.astype(jnp.float32)).astype(jnp.bfloat16) for value, high in zip(values, highs)]
+    main = layout.main
+    left = jnp.concatenate(highs[:main] + lows[:main] + highs[main:] + lows[main:], axis=1)
+    both = jnp.dot(left, table_ref[...], preferred_element_type=jnp.float32)
+    return both[:, :LAGS] + both[:, LAGS:]
 
 
 def near_kernel(layout, pieces_ref, sums_ref, table_ref, own_ref, rest_ref, partner, anchors):
@@ -254,9 +271,9 @@
         functools.partial(near_kernel, layout),
         out_shape=(
             pltpu.VMEM((layout.rows, LAGS), jnp.float32),
-            pltpu.VMEM((layout.depth, 2 * LAGS), jnp.bfloat16),
+            pltpu.VMEM((2 * layout.depth, 2 * LAGS), jnp.bfloat16),
             pltpu.VMEM((bands * layout.stations * ROWS, LANES), jnp.float32),
-            pltpu.VMEM((2 * bands * layout.stations * COMPONENTS, LANES), jnp.float32),
+            pltpu.VMEM((2 * layout.tails * layout.stations * COMPONENTS, LANES), jnp.float32),
         ),
         in_specs=[vmem],
         out_specs=(vmem,) * 4,

time: 14.9 us -> 14.9 us (level)
  transfers between devices with their start and end apart: 1 -> 1, of which waited for: 1 -> 1; matrix products, arithmetic and copies ran while one was open for 0% -> 0% of each run, Pallas kernels for 4% -> 3%
where the time goes in v6:
time: 14.9 us; the launch traced here: 14.7 us
  blocking collectives  11.5 us (77%)
  Pallas kernels  2.19 us (15%)
  starting transfers between devices  0.57 us (4%)
  waiting for transfers between devices  0.37 us (2%)
    all_to_all x1, blocking collectives, body(): lax.all_to_all(pieces, ('blk', 'band'), split_axis=0, concat_axis=0, tile...  11.5 us
    pallas_call x1, Pallas kernels, body(): pl.pallas_call(functools.partial(far_kernel, layout), out_shape=jax.Shape...  0.92 us
    pallas_call x1, Pallas kernels, body(): pl.pallas_call(functools.partial(pack_kernel, layout), out_shape=pltpu.VM...  0.79 us
    ppermute x1, starting transfers between devices, body(): lax.ppermute(near[:, :ROWS], 'blk', [(i, i ^ 1) for i in range(peers)])  0.57 us
    pallas_call x1, Pallas kernels, body(): pl.pallas_call(functools.partial(near_kernel, layout), out_shape=(pltpu.V...  0.48 us
    ppermute x1, waiting for transfers between devices, body(): lax.ppermute(near[:, :ROWS], 'blk', [(i, i ^ 1) for i in range(peers)])  0.37 us
  transfers between devices with their start and end apart: 1, of which 1 were waited for; matrix products, arithmetic and copies ran while one was open for 0% of the time, Pallas kernels for 3%

profile of v6, /device:TPU:0, one launch (start us, length us, event | category | flops | bytes accessed | tf_op | source)
XLA Modules:
  0.0 14.7 jit_solution(17843769864383578962)
XLA Ops:
  0.0 0.8 %pack.1 = bf16[16,16,128]{2,1,0:T(8,128)(2,1)S(1)} custom-call(s32[2,3]{1,0:T(2,128)} %quality_ref.1, bf16[2,3,2,160]{3,2,1,0:T(2,128)(2,1)} %spectra_ref.1), custom_call_target="tpu_custom_call" | custom-call | tf_op jit(solution)/shard_map/pack/pallas_call | solution.py:251
  0.8 11.5 %all_to_all.5.pieces_ref = bf16[16,16,128]{2,1,0:T(8,128)(2,1)S(1)} all-to-all(bf16[16,16,128]{2,1,0:T(8,128)(2,1)S(1)} %pack.1), channel_id=1, replica_groups={{29,2,3,6,7,10,11,14,15,16,17,20,21,24,25,28},{31,0,1,4,5,8,9,12,13,18,..., dimensions={0} | all-to-all | bytes 131072 | tf_op jit(solution)/shard_map/all_to_all | solution.py:265
  12.3 0.6 %collective-permute-start = (bf16[16,8,128]{2,1,0:T(8,128)(2,1)S(1)}, bf16[16,8,128]{2,1,0:T(8,128)(2,1)S(1)}, u32[]{:S(2)}, u32[]{:S(2)}) collective-permute-start(bf16[16,8,128]{2,1,0:T(8,128)(2,1)S(1)} %slice.4), channel_id=1, source_target_pairs={{0,2},{2,0},{4,6},{6,4},{8,10},{10,8},{12,14},{14,12},{16,18},{18,... | collective-permute-start | bytes 98312 | tf_op jit(solution)/shard_map/ppermute | solution.py:268
  12.9 0.5 %near.1 = (f32[144,128]{1,0:T(8,128)S(1)}, bf16[1280,256]{1,0:T(8,128)(2,1)S(1)}, f32[32,128]{1,0:T(8,128)S(1)}, f32[12,128]{1,0:T(8,128)S(1)}) custom-call(bf16[16,16,128]{2,1,0:T(8,128)(2,1)S(1)} %all_to_all.5.pieces_ref), custom_call_target="tpu_custom_call" | custom-call | flops 100000000 | bytes 1000000 | tf_op jit(solution)/shard_map/near/pallas_call | solution.py:270
  13.4 0.4 %collective-permute-done.pieces_ref = bf16[16,8,128]{2,1,0:T(8,128)(2,1)S(1)} collective-permute-done((bf16[16,8,128]{2,1,0:T(8,128)(2,1)S(1)}, bf16[16,8,128]{2,1,0:T(8,128)(2,1)S(1)}, u32[]{:S(2)}, u32[]{:S(2)}) %collective-permute-start) | collective-permute-done | bytes 32800 | tf_op jit(solution)/shard_map/ppermute | solution.py:268
  13.7 0.9 %far.1 = bf16[288,128]{1,0:T(8,128)(2,1)} custom-call(bf16[16,8,128]{2,1,0:T(8,128)(2,1)S(1)} %collective-permute-done.pieces_ref, f32[144,128]{1,0:T(8,128)S(1)} %get-tuple-element.9.near_ref, bf16[1280,256]{1,0:T(8,128)(2,1)S(1)} %get-tuple-element.10.table_ref, f32[32,128]{1,0:T(8,128)S(1)} %get-tuple-element.11.own_ref, ...), custom_call_target="tpu_custom_call" | custom-call | tf_op jit(solution)/shard_map/far/pallas_call | solution.py:288
  (1 shorter events, 0.0 us)
Async XLA Ops:
  12.3 1.4 %collective-permute-start = (bf16[16,8,128]{2,1,0:T(8,128)(2,1)S(1)}, bf16[16,8,128]{2,1,0:T(8,128)(2,1)S(1)}, u32[]{:S(2)}, u32[]{:S(2)}) collective-permute-start(bf16[16,8,128]{2,1,0:T(8,128)(2,1)S(1)} %slice.4), channel_id=1, source_target_pairs={{0,2},{2,0},{4,6},{6,4},{8,10},{10,8},{12,14},{14,12},{16,18},{18,... | collective-permute-start | bytes 98312 | tf_op jit(solution)/shard_map/ppermute | solution.py:268

commit v7 on v6

--- a/solution.py
+++ b/solution.py
@@ -57,19 +57,24 @@
 
 def pack_kernel(layout, quality_ref, spectra_ref, pieces_ref, wide):
     stations = layout.stations
+    spare = jnp.zeros((2, LANES - layout.rest), jnp.float32)
+    raw = []
+    for s in range(stations):
+        for a in range(COMPONENTS):
+            both = spectra_ref[s * COMPONENTS + a].astype(jnp.float32)
+            rest = jnp.concatenate([both[:, layout.whole * LANES :], spare], axis=1)
+            raw.append((both, pltpu.roll(rest, a * layout.rest, 1) if a else rest))
     if layout.rest_row + 2 < ROWS:
         wide[...] = jnp.zeros_like(wide)
     for s in range(stations):
-        rests = jnp.zeros((2, LANES), jnp.float32)
+        rests = None
         for a in range(COMPONENTS):
             usable = quality_ref[s, a].astype(jnp.float32)
-            both = spectra_ref[s, a].astype(jnp.float32) * usable
+            both, rest = raw[s * COMPONENTS + a]
             for chunk in range(layout.whole):
-                row = s * ROWS + 2 * (a * layout.whole + chunk)
-                wide[row : row + 2, :] = both[:, chunk * LANES : (chunk + 1) * LANES]
-            rest = both[:, layout.whole * LANES :]
-            padded = jnp.concatenate([rest, jnp.zeros((2, LANES - layout.rest), jnp.float32)], axis=1)
-            rests = rests + (pltpu.roll(padded, a * layout.rest, 1) if a else padded)
+                row = s * ROWS + layout.row(a, chunk)
+                wide[row : row + 2, :] = both[:, chunk * LANES : (chunk + 1) * LANES] * usable
+            rests = rest * usable if rests is None else rests + rest * usable
         row = s * ROWS + layout.rest_row
         wide[row : row + 2, :] = rests
     packed = [wide[s * ROWS : (s + 1) * ROWS, :] for s in range(stations)]
@@ -255,7 +260,7 @@
         out_specs=vmem,
         scratch_shapes=[pltpu.VMEM((piece_rows, LANES), jnp.float32)],
         name="pack",
-    )(quality, spectra)
+    )(quality, spectra.reshape(-1, 2, spectra.shape[3]))
     groups = [[0] * layout.slots for _ in range(CORES)]
     for half in range(layout.halves):
         for core in range(CORES):

time: 14.9 us -> 14.9 us (level)
  no operation moved by 1% of the time
where the time goes in v7:
time: 14.9 us; the launch traced here: 14.7 us
  blocking collectives  11.5 us (77%)
  Pallas kernels  2.19 us (15%)
  starting transfers between devices  0.57 us (4%)
  waiting for transfers between devices  0.37 us (2%)
    all_to_all x1, blocking collectives, body(): lax.all_to_all(pieces, ('blk', 'band'), split_axis=0, concat_axis=0, tile...  11.5 us
    pallas_call x1, Pallas kernels, body(): pl.pallas_call(functools.partial(far_kernel, layout), out_shape=jax.Shape...  0.92 us
    pallas_call x1, Pallas kernels, body(): pl.pallas_call(functools.partial(pack_kernel, layout), out_shape=pltpu.VM...  0.79 us
    ppermute x1, starting transfers between devices, body(): lax.ppermute(near[:, :ROWS], 'blk', [(i, i ^ 1) for i in range(peers)])  0.57 us
    pallas_call x1, Pallas kernels, body(): pl.pallas_call(functools.partial(near_kernel, layout), out_shape=(pltpu.V...  0.48 us
    ppermute x1, waiting for transfers between devices, body(): lax.ppermute(near[:, :ROWS], 'blk', [(i, i ^ 1) for i in range(peers)])  0.37 us
  transfers between devices with their start and end apart: 1, of which 1 were waited for; matrix products, arithmetic and copies ran while one was open for 0% of the time, Pallas kernels for 3%

profile of v7, /device:TPU:0, one launch (start us, length us, event | category | flops | bytes accessed | tf_op | source)
XLA Modules:
  0.0 14.7 jit_solution(643409768635323056)
XLA Ops:
  0.0 0.8 %pack.1 = bf16[16,16,128]{2,1,0:T(8,128)(2,1)S(1)} custom-call(s32[2,3]{1,0:T(2,128)} %quality_ref.1, bf16[6,2,160]{2,1,0:T(2,128)(2,1)} %bitcast.6), custom_call_target="tpu_custom_call" | custom-call | tf_op jit(solution)/shard_map/pack/pallas_call | solution.py:256
  0.8 11.5 %all_to_all.5.pieces_ref = bf16[16,16,128]{2,1,0:T(8,128)(2,1)S(1)} all-to-all(bf16[16,16,128]{2,1,0:T(8,128)(2,1)S(1)} %pack.1), channel_id=1, replica_groups={{29,2,3,6,7,10,11,14,15,16,17,20,21,24,25,28},{31,0,1,4,5,8,9,12,13,18,..., dimensions={0} | all-to-all | bytes 131072 | tf_op jit(solution)/shard_map/all_to_all | solution.py:270
  12.3 0.6 %collective-permute-start = (bf16[16,8,128]{2,1,0:T(8,128)(2,1)S(1)}, bf16[16,8,128]{2,1,0:T(8,128)(2,1)S(1)}, u32[]{:S(2)}, u32[]{:S(2)}) collective-permute-start(bf16[16,8,128]{2,1,0:T(8,128)(2,1)S(1)} %slice.4), channel_id=1, source_target_pairs={{0,2},{2,0},{4,6},{6,4},{8,10},{10,8},{12,14},{14,12},{16,18},{18,... | collective-permute-start | bytes 98312 | tf_op jit(solution)/shard_map/ppermute | solution.py:273
  12.9 0.5 %near.1 = (f32[144,128]{1,0:T(8,128)S(1)}, bf16[1280,256]{1,0:T(8,128)(2,1)S(1)}, f32[32,128]{1,0:T(8,128)S(1)}, f32[12,128]{1,0:T(8,128)S(1)}) custom-call(bf16[16,16,128]{2,1,0:T(8,128)(2,1)S(1)} %all_to_all.5.pieces_ref), custom_call_target="tpu_custom_call" | custom-call | flops 100000000 | bytes 1000000 | tf_op jit(solution)/shard_map/near/pallas_call | solution.py:275
  13.4 0.4 %collective-permute-done.pieces_ref = bf16[16,8,128]{2,1,0:T(8,128)(2,1)S(1)} collective-permute-done((bf16[16,8,128]{2,1,0:T(8,128)(2,1)S(1)}, bf16[16,8,128]{2,1,0:T(8,128)(2,1)S(1)}, u32[]{:S(2)}, u32[]{:S(2)}) %collective-permute-start) | collective-permute-done | bytes 32800 | tf_op jit(solution)/shard_map/ppermute | solution.py:273
  13.7 0.9 %far.1 = bf16[288,128]{1,0:T(8,128)(2,1)} custom-call(bf16[16,8,128]{2,1,0:T(8,128)(2,1)S(1)} %collective-permute-done.pieces_ref, f32[144,128]{1,0:T(8,128)S(1)} %get-tuple-element.9.near_ref, bf16[1280,256]{1,0:T(8,128)(2,1)S(1)} %get-tuple-element.10.table_ref, f32[32,128]{1,0:T(8,128)S(1)} %get-tuple-element.11.own_ref, ...), custom_call_target="tpu_custom_call" | custom-call | tf_op jit(solution)/shard_map/far/pallas_call | solution.py:293
  (1 shorter events, 0.0 us)
Async XLA Ops:
  12.3 1.4 %collective-permute-start = (bf16[16,8,128]{2,1,0:T(8,128)(2,1)S(1)}, bf16[16,8,128]{2,1,0:T(8,128)(2,1)S(1)}, u32[]{:S(2)}, u32[]{:S(2)}) collective-permute-start(bf16[16,8,128]{2,1,0:T(8,128)(2,1)S(1)} %slice.4), channel_id=1, source_target_pairs={{0,2},{2,0},{4,6},{6,4},{8,10},{10,8},{12,14},{14,12},{16,18},{18,... | collective-permute-start | bytes 98312 | tf_op jit(solution)/shard_map/ppermute | solution.py:273
